TPU v7x, 256 devices: a whole 4x4x8 slice. The times are simulated.
256 devices in a mesh: dp: 4 (over x_hi, core), seq: 64 (over x_lo, y, z).
Axes of the slice: x: 4 (x_hi: 2, x_lo: 2; x = x_hi * 2 + x_lo), y: 4, z: 8, core: 2. Of those that a mesh axis runs over, the one named last changes fastest.
Arguments:
- ids: int32 [4, 8192], P('dp', 'seq'), may hold values from 0 to 511
- embed: bfloat16 [512, 2048], replicated, may hold values from -6 to 6
- weight: bfloat16 [2048, 2048], P('seq'), may hold values from -0.125 to 0.125
- filters: float32 [2048, 8192], P('seq'), may hold values from -4 to 4
- out_grad: bfloat16 [4, 8192, 2048], P('dp', 'seq'), may hold values from -6 to 6
- momentum: float32 [4, 2048, 2048], P('dp', 'seq'), may hold values from -8 to 8
- feedback: float32 [4, 2048, 2048], P('dp', 'seq'), may hold values from -4 to 4
Outputs:
- output: bfloat16 [4, 8192, 2048], P('dp', 'seq')
- new_momentum: float32 [4, 2048, 2048], P('dp', 'seq')
- new_feedback: float32 [4, 2048, 2048], P('dp', 'seq')
- new_weight: bfloat16 [2048, 2048], P('seq')
All inputs are finite; a program needn't handle non-finite values. Where the computation divides by a largest or mean magnitude, that divisor is 1e-20 or more.
Results may differ from a plain program's by a relative error of at most 0.008.
Values may be sent and summed in bfloat16 or wider, within the bound.
No kernel may reach another device: no remote copies, remote signals or barrier semaphores. Data moves between devices by JAX's collectives and lax.ppermute only.
A program may use at most 128 MiB of HBM per device.

v0:
```python
import math

import jax
import jax.numpy as jnp
from jax import lax
from jax.sharding import PartitionSpec as P

momentum_keep = 0.9
step_rate = 0.02
tiny_shift = 1e-06


def angle_table(left, right, period):
    product = left[:, None] * right[None, :] % period
    phase = product.astype(jnp.float32) * (-2.0 * math.pi / period)
    return (jnp.cos(phase), jnp.sin(phase))


def make_tables(total_len):
    first = 128
    second = total_len // first
    first_index = lax.iota(jnp.int32, first)
    second_index = lax.iota(jnp.int32, second)
    return (
        angle_table(first_index, first_index, first),
        angle_table(second_index, second_index, second),
        angle_table(first_index, second_index, total_len),
    )


def forward_transform(signal, tables):
    (first_real, first_imag), (second_real, second_imag), (twist_real, twist_imag) = tables
    grid = signal.reshape(signal.shape[0], first_real.shape[0], second_real.shape[0])
    outer_real = jnp.einsum("ca,jab->jcb", first_real, grid, precision=lax.Precision.HIGHEST)
    outer_imag = jnp.einsum("ca,jab->jcb", first_imag, grid, precision=lax.Precision.HIGHEST)
    turned_real = outer_real * twist_real - outer_imag * twist_imag
    turned_imag = outer_real * twist_imag + outer_imag * twist_real
    spec_real = jnp.einsum(
        "jcb,bd->jcd", turned_real, second_real, precision=lax.Precision.HIGHEST
    ) - jnp.einsum("jcb,bd->jcd", turned_imag, second_imag, precision=lax.Precision.HIGHEST)
    spec_imag = jnp.einsum(
        "jcb,bd->jcd", turned_real, second_imag, precision=lax.Precision.HIGHEST
    ) + jnp.einsum("jcb,bd->jcd", turned_imag, second_real, precision=lax.Precision.HIGHEST)
    return (spec_real, spec_imag)


def inverse_transform(spec_real, spec_imag, tables, length):
    (first_real, first_imag), (second_real, second_imag), (twist_real, twist_imag) = tables
    inner_real = jnp.einsum(
        "jcd,db->jcb", spec_real, second_real, precision=lax.Precision.HIGHEST
    ) + jnp.einsum("jcd,db->jcb", spec_imag, second_imag, precision=lax.Precision.HIGHEST)
    inner_imag = jnp.einsum(
        "jcd,db->jcb", spec_imag, second_real, precision=lax.Precision.HIGHEST
    ) - jnp.einsum("jcd,db->jcb", spec_real, second_imag, precision=lax.Precision.HIGHEST)
    turned_real = inner_real * twist_real + inner_imag * twist_imag
    turned_imag = inner_imag * twist_real - inner_real * twist_imag
    values = jnp.einsum(
        "ac,jcb->jab", first_real, turned_real, precision=lax.Precision.HIGHEST
    ) + jnp.einsum("ac,jcb->jab", first_imag, turned_imag, precision=lax.Precision.HIGHEST)
    total_len = first_real.shape[0] * second_real.shape[0]
    return values.reshape(values.shape[0], total_len)[:, :length] * (1.0 / total_len)


def channel_filter(block, spectrum, tables, mirror):
    length = block.shape[0]
    signal = jnp.pad(block.astype(jnp.float32).T, ((0, 0), (0, length)))
    sig_real, sig_imag = forward_transform(signal, tables)
    filt_real = spectrum[0]
    filt_imag = mirror * spectrum[1]
    prod_real = sig_real * filt_real - sig_imag * filt_imag
    prod_imag = sig_real * filt_imag + sig_imag * filt_real
    return inverse_transform(prod_real, prod_imag, tables, length).T.astype(jnp.bfloat16)


def per_device(ids, embed, weight, filters, out_grad, momentum, feedback):
    parts = lax.axis_size("seq")
    vocab = embed.shape[0]
    tokens_here = ids.shape[1]
    length = tokens_here * parts
    picks = (ids[0][:, None] == lax.iota(jnp.int32, vocab)[None, :]).astype(jnp.bfloat16)
    inputs = jnp.dot(picks, embed, preferred_element_type=jnp.float32).astype(jnp.bfloat16)
    columns = inputs
    projected = jnp.dot(
        columns,
        lax.all_gather(weight, "seq", axis=0, tiled=True),
        preferred_element_type=jnp.float32,
    ).astype(jnp.bfloat16)
    upstream = (out_grad[0].astype(jnp.float32) * inputs.astype(jnp.float32)).astype(jnp.bfloat16)
    tables = make_tables(2 * length)
    spectrum = forward_transform(jnp.pad(filters, ((0, 0), (0, length))), tables)
    proj_cols = lax.all_to_all(projected, "seq", split_axis=1, concat_axis=0, tiled=True)
    convolved = lax.all_to_all(
        channel_filter(proj_cols, spectrum, tables, 1.0),
        "seq",
        split_axis=0,
        concat_axis=1,
        tiled=True,
    )
    up_cols = lax.all_to_all(upstream, "seq", split_axis=1, concat_axis=0, tiled=True)
    back_cols = channel_filter(up_cols, spectrum, tables, -1.0)
    output = (inputs.astype(jnp.float32) * convolved.astype(jnp.float32)).astype(jnp.bfloat16)
    scaling = 1.0 / math.sqrt(length)
    downstream = lax.all_to_all(back_cols, "seq", split_axis=0, concat_axis=1, tiled=True)
    columns = inputs
    gradient = (
        lax.psum_scatter(
            jnp.dot(columns.T, downstream, preferred_element_type=jnp.float32),
            "seq",
            scatter_dimension=0,
            tiled=True,
        )
        * scaling
    )
    updated = momentum_keep * momentum[0] + (1.0 - momentum_keep) * gradient
    combined = updated + feedback[0]
    scale = jnp.mean(jnp.abs(combined), axis=1, keepdims=True) + tiny_shift
    quantized = (scale * jnp.clip(combined / scale, -1.0, 1.0)).astype(jnp.bfloat16)
    residue = combined - quantized.astype(jnp.float32)
    summed = lax.psum(quantized.astype(jnp.float32).astype(jnp.bfloat16), "dp").astype(jnp.float32)
    average = summed / lax.axis_size("dp")
    new_weight = (weight.astype(jnp.float32) - step_rate * average).astype(jnp.bfloat16)
    return (output[None], updated[None], residue[None], new_weight)


def solution(mesh):
    placed = (
        P("dp", "seq"),
        P(),
        P("seq", None),
        P("seq", None),
        P("dp", "seq", None),
        P("dp", "seq", None),
        P("dp", "seq", None),
    )
    return jax.shard_map(
        per_device,
        mesh=mesh,
        in_specs=placed,
        out_specs=(
            P("dp", "seq", None),
            P("dp", "seq", None),
            P("dp", "seq", None),
            P("seq", None),
        ),
        check_vma=False,
    )
```

profile of v0, /device:TPU:6, one launch (start us, length us, event | category | flops | bytes accessed | tf_op | source)
XLA Modules:
  0.0 836.0 jit_solution(6435790167755759615)
XLA Ops:
  11.3 13.2 %all-to-all-start.2 = ((bf16[128,64,32]{0,2,1:T(8,128)(2,1)}), bf16[128,64,32]{0,2,1:T(8,128)(2,1)S(1)}, u32[]{:S(2)}, u32[]{:S(2)}) async-start(bf16[128,64,32]{0,2,1:T(8,128)(2,1)} %bitcast.17), calls=%async_computation.2 | async-start | bytes 1048576 | tf_op jit(solution)/shard_map/all_to_all | solution.py:99
  28.4 5.3 fusion.78
  37.4 4.0 fusion.48
  41.4 3.8 fusion.46
  45.1 5.1 convolution_subtract_fusion.3
  50.2 5.0 convolution_add_fusion.3
  55.6 13.3 %fusion.70 = f32[32,128,128]{2,1,0:T(8,128)S(1)} fusion(bf16[32,128,128]{2,1,0:T(8,128)(2,1)S(1)} %bitcast.232), kind=kOutput, calls=%fused_computation.109 | convolution fusion | flops 805535744 | bytes 3145728 | tf_op jit(solution)/shard_map/ca,jab->jcb/dot_general | solution.py:35
  71.7 255.4 %all-gather.2.cloned.1.call-done = bf16[2048,2048]{1,0:T(8,128)(2,1)} async-done(((bf16[32,2048]{1,0:T(8,128)(2,1)}), bf16[2048,2048]{1,0:T(8,128)(2,1)}) %all-gather.2.cloned.1.call-update) | async-done | bytes 8388624 | tf_op jit(solution)/shard_map/all_gather | solution.py:85
  327.1 4.6 convolution_convert_fusion
  332.8 7.4 all-to-all-start
  340.3 5.5 fusion.54
  345.8 5.0 fusion.52
  350.7 5.0 convolution_subtract_fusion.1
  359.5 3.8 fusion.40
  363.2 3.7 fusion.42
  367.0 3.9 convolution_add_fusion.4
  371.0 3.8 convolution_subtract_fusion.4
  374.8 6.4 multiply_add_fusion
  392.6 3.8 add_bitcast_fusion
  399.7 25.7 %all_to_all.58 = bf16[64,128,32]{1,2,0:T(8,128)(2,1)S(1)} all-to-all(bf16[64,128,32]{1,2,0:T(8,128)(2,1)S(1)} %copy_bitcast_fusion.2), channel_id=1, replica_groups=mesh['dp'=4,'seq'=64] {'seq'}, dimensions={0} | all-to-all | bytes 1048576 | tf_op jit(solution)/shard_map/all_to_all | solution.py:103
  425.3 8.1 fusion.266
  453.2 24.7 %all_to_all.59 = bf16[64,128,32]{1,2,0:T(8,128)(2,1)S(1)} all-to-all(bf16[64,128,32]{1,2,0:T(8,128)(2,1)S(1)} %copy_bitcast_fusion.3), channel_id=1, replica_groups=mesh['dp'=4,'seq'=64] {'seq'}, dimensions={0} | all-to-all | bytes 1048576 | tf_op jit(solution)/shard_map/all_to_all | solution.py:92
  481.8 302.3 %reduce-scatter.2.cloned.1.call-done = f32[32,2048]{1,0:T(8,128)} async-done(((f32[2048,2048]{1,0:T(8,128)}), f32[32,2048]{1,0:T(8,128)}) %reduce-scatter.2.cloned.1.call-update) | async-done | bytes 262160 | tf_op jit(solution)/shard_map/reduce_scatter | solution.py:106
  788.9 38.6 %all-reduce.5.cloned.1.call-done = bf16[32,2048]{1,0:T(8,128)(2,1)} async-done(((bf16[32,2048]{1,0:T(8,128)(2,1)}), bf16[32,2048]{1,0:T(8,128)(2,1)}) %all-reduce.5.cloned.1.call-update) | async-done | bytes 131088 | tf_op jit(solution)/shard_map/psum | solution.py:119
  (79 shorter events, 63.9 us)
Async XLA Ops:
  7.2 1.6 copy-start
  7.2 320.0 %all-gather.2.cloned.1.call-start = ((), (), s32[]{:S(2)}) async-start(), calls=%async_computation.5 | async-start | bytes 8519680 | tf_op jit(solution)/shard_map/all_gather | solution.py:85
  11.3 44.0 %all-to-all-start.2 = ((bf16[128,64,32]{0,2,1:T(8,128)(2,1)}), bf16[128,64,32]{0,2,1:T(8,128)(2,1)S(1)}, u32[]{:S(2)}, u32[]{:S(2)}) async-start(bf16[128,64,32]{0,2,1:T(8,128)(2,1)} %bitcast.17), calls=%async_computation.2 | async-start | bytes 1048576 | tf_op jit(solution)/shard_map/all_to_all | solution.py:99
  28.4 5.3 copy-start.6
  332.8 23.0 %all-to-all-start = ((bf16[128,64,32]{0,2,1:T(8,128)(2,1)}), bf16[128,64,32]{0,2,1:T(8,128)(2,1)S(1)}, u32[]{:S(2)}, u32[]{:S(2)}) async-start(bf16[128,64,32]{0,2,1:T(8,128)(2,1)} %bitcast.242), calls=%async_computation | async-start | bytes 1048576 | tf_op jit(solution)/shard_map/all_to_all | solution.py:91
  340.2 443.8 %reduce-scatter.2.cloned.1.call-start = ((), (), s32[]{:S(2)}) async-start(), calls=%async_computation.6 | async-start | bytes 17039360 | tf_op jit(solution)/shard_map/reduce_scatter | solution.py:106
  340.3 5.5 copy-start.2
  367.0 7.8 copy-start.10
  370.9 3.9 copy-start.3
  370.9 3.9 copy-start.7
  371.0 3.9 copy-start.8
  371.0 3.9 copy-start.9
  433.4 1.6 copy-start.4
  433.4 394.1 %all-reduce.5.cloned.1.call-start = ((), (), s32[]{:S(2)}) async-start(), calls=%async_computation.7 | async-start | bytes 262144 | tf_op jit(solution)/shard_map/psum | solution.py:119
  435.0 2.3 copy-start.5
  478.0 306.1 %copy-start.12 = (f32[1,32,2048]{2,1,0:T(8,128)S(1)}, f32[1,32,2048]{2,1,0:T(8,128)}, u32[]{:S(2)}) copy-start(f32[1,32,2048]{2,1,0:T(8,128)} %param.13) | copy-start | bytes 786436
  478.0 306.1 %copy-start.13 = (f32[1,32,2048]{2,1,0:T(8,128)S(1)}, f32[1,32,2048]{2,1,0:T(8,128)}, u32[]{:S(2)}) copy-start(f32[1,32,2048]{2,1,0:T(8,128)} %param.12) | copy-start | bytes 786436
  479.1 350.1 %copy-start.1 = (bf16[512,2048]{1,0:T(8,128)(2,1)S(1)}, bf16[512,2048]{1,0:T(8,128)(2,1)}, u32[]{:S(2)}) copy-start(bf16[512,2048]{1,0:T(8,128)(2,1)} %param.8) | copy-start | bytes 6291460
  481.8 345.8 %copy-start.11 = (bf16[32,2048]{1,0:T(8,128)(2,1)S(1)}, bf16[32,2048]{1,0:T(8,128)(2,1)}, u32[]{:S(2)}) copy-start(bf16[32,2048]{1,0:T(8,128)(2,1)} %param.9) | copy-start | bytes 393220
Sparse Core Ops, SparseCore 0:
  9.8 317.2 all-gather.1
  433.6 350.4 reduce-scatter.1
  787.3 40.2 all-reduce.4
where the time goes:
time: 849 us; the launch traced here: 836 us
  waiting for transfers between devices  597 us (70%)
  matrix products  128 us (15%)
  blocking collectives  50.4 us (6%)
  starting transfers between devices  20.7 us (2%)
  local copies, waits for them, and re-layouts  17.4 us (2%)
  between operations  14.6 us (2%)
    reduce_scatter x1, waiting for transfers between devices, per_device(): lax.psum_scatter(jnp.dot(columns.T, downstream, preferred_element_type=jn...  302 us
    all_gather x1, waiting for transfers between devices, per_device(): lax.all_gather(weight, 'seq', axis=0, tiled=True)  255 us
    psum x1, waiting for transfers between devices, per_device(): lax.psum(quantized.astype(jnp.float32).astype(jnp.bfloat16), 'dp')  38.6 us
    all_to_all x1, blocking collectives, per_device(): lax.all_to_all(back_cols, 'seq', split_axis=0, concat_axis=1, tiled=True)  25.7 us
    all_to_all x1, blocking collectives, per_device(): lax.all_to_all(channel_filter(proj_cols, spectrum, tables, 1.0), 'seq', s...  24.7 us
    dot_general x3, matrix products, forward_transform(): jnp.einsum('ca,jab->jcb', first_imag, grid, precision=lax.Precision.HIGHEST)  20.5 us
  transfers between devices with their start and end apart: 5, of which 3 were waited for; matrix products, arithmetic and copies ran while one was open for 11% of the time, Pallas kernels for 0%

commit v1 on v0

v1 whole, which is shorter than its diff:
```python
import functools
import math

import jax
import jax.numpy as jnp
import numpy as np
from jax import lax
from jax.experimental import pallas as pl
from jax.experimental.pallas import tpu as pltpu
from jax.sharding import PartitionSpec as P

momentum_keep = 0.9
step_rate = 0.02
tiny_shift = 1e-06

F32 = jnp.float32
BF16 = jnp.bfloat16
LANES = 128
GROUP = 8
HALVES = 4
SIDE = 32
VMEM_LIMIT = 44 * 1024 * 1024


def split_const(table):
    high = np.asarray(table, np.float32).astype(BF16)
    low = (table - high.astype(np.float64)).astype(np.float32).astype(BF16)
    return high, low


def transform_tables(outer, inner):
    total = outer * inner
    freq = np.arange(outer)[:, None] + 0.25
    first = np.exp(-2j * np.pi * freq * np.arange(outer)[None, :] / outer)
    twist = np.exp(-2j * np.pi * freq * np.arange(inner)[None, :] / total)
    second = np.exp(
        -2j * np.pi * (np.arange(inner)[:, None] * np.arange(inner)[None, :] % inner) / inner
    )
    stage = np.concatenate([first.real, first.imag], axis=0)
    high, low = split_const(stage)
    back_high, back_low = split_const(stage.T)
    real, imag = second.real, second.imag
    mix = np.block([[real, imag], [-imag, real]])
    unmix = np.block([[real, -imag], [imag, real]])
    return {
        "exact": np.concatenate([high, low], axis=1),
        "wide": np.concatenate([high, high, low], axis=1),
        "back": np.concatenate([back_high, back_high, back_low], axis=1),
        "twist": np.concatenate([twist.real, twist.imag], axis=1).astype(np.float32),
        "mix": np.stack(split_const(mix)),
        "unmix": np.stack(split_const(unmix)),
    }


def mm(left, right):
    return jnp.dot(left, right, preferred_element_type=F32)


def halves(values):
    high = values.astype(BF16)
    return high, (values - high.astype(F32)).astype(BF16)


def mm_wide(values, table_ref):
    rows = values.shape[0]
    high, low = halves(values)
    both = mm(jnp.concatenate([high, low], axis=0), table_ref[0])
    return both[:rows] + both[rows:] + mm(high, table_ref[1])


def spread(columns, stage_ref, twist_ref, exact):
    real_twist = twist_ref[:, :LANES]
    imag_twist = twist_ref[:, LANES:]
    outer = real_twist.shape[0]
    rows = []
    for first in range(0, len(columns), 2):
        pair = jnp.concatenate(columns[first : first + 2], axis=1)
        if exact:
            high = pair.astype(BF16)
            stack = jnp.concatenate([high, high], axis=0)
        else:
            high, low = halves(pair)
            stack = jnp.concatenate([high, low, high], axis=0)
        grid = mm(stage_ref[...], stack)
        for which in range(2):
            lane = slice(which * LANES, (which + 1) * LANES)
            real = grid[:outer, lane]
            imag = grid[outer:, lane]
            rows.append(
                jnp.concatenate(
                    [
                        real * real_twist - imag * imag_twist,
                        real * imag_twist + imag * real_twist,
                    ],
                    axis=1,
                )
            )
    return jnp.concatenate(rows, axis=0)


def gather_back(spectrum, back_ref, twist_ref):
    real_twist = twist_ref[:, :LANES]
    imag_twist = twist_ref[:, LANES:]
    outer = real_twist.shape[0]
    count = spectrum.shape[0] // outer
    turned = []
    for which in range(count):
        real = spectrum[which * outer : (which + 1) * outer, :LANES]
        imag = spectrum[which * outer : (which + 1) * outer, LANES:]
        turned.append(
            jnp.concatenate(
                [
                    real * real_twist + imag * imag_twist,
                    imag * real_twist - real * imag_twist,
                ],
                axis=0,
            )
        )
    columns = []
    for first in range(0, count, 2):
        high, low = halves(jnp.concatenate(turned[first : first + 2], axis=1))
        pair = mm(back_ref[...], jnp.concatenate([high, low, high], axis=0))
        columns += [pair[:, :LANES], pair[:, LANES:]]
    return columns


def spectrum_kernel(filters_ref, wide_ref, twist_ref, mix_ref, out_ref):
    channels, outer, _ = filters_ref.shape
    norm = 1.0 / (outer * LANES)

    @pl.loop(0, channels // GROUP)
    def _(step):
        columns = [filters_ref[step * GROUP + k] * norm for k in range(GROUP)]
        rows = spread(columns, wide_ref, twist_ref, False)
        span = GROUP * outer
        out_ref[pl.ds(pl.multiple_of(step * span, span), span), :] = mm_wide(rows, mix_ref)


def convolve(values_ref, spectrum_ref, tables, sign):
    exact_ref, twist_ref, mix_ref, unmix_ref, back_ref = tables
    outer = twist_ref.shape[0]
    channels = values_ref.shape[0] // outer
    span = GROUP * outer

    @pl.loop(0, channels // GROUP)
    def _(step):
        base = step * GROUP
        columns = [
            values_ref[pl.ds(base + k, outer, stride=channels), :] for k in range(GROUP)
        ]
        bins = mm_wide(spread(columns, exact_ref, twist_ref, True), mix_ref)
        filt = spectrum_ref[pl.ds(pl.multiple_of(step * span, span), span), :]
        real, imag = bins[:, :LANES], bins[:, LANES:]
        filt_real, filt_imag = filt[:, :LANES], filt[:, LANES:]
        product = jnp.concatenate(
            [
                real * filt_real - sign * (imag * filt_imag),
                imag * filt_real + sign * (real * filt_imag),
            ],
            axis=1,
        )
        result = gather_back(mm_wide(product, unmix_ref), back_ref, twist_ref)
        for k in range(GROUP):
            values_ref[pl.ds(base + k, outer, stride=channels), :] = result[k]


def one_hot_columns(ids, vocab):
    match = lax.broadcasted_iota(jnp.int32, (vocab, ids.shape[1]), 0) == ids
    return jnp.where(match, 1.0, 0.0).astype(BF16)


def swap_blocks(parts):
    lane = lax.broadcasted_iota(jnp.int32, parts[0].shape, 1) // SIDE
    out = []
    for to in range(HALVES):
        total = None
        for source in range(HALVES):
            moved = parts[source]
            if source != to:
                moved = pltpu.roll(moved, ((source - to) * SIDE) % LANES, 1)
            total = moved if total is None else jnp.where(lane == source, moved, total)
        out.append(total)
    return out


def send_kernel(ids_ref, ids_col_ref, embed_ref, weight_ref, grad_ref, inputs_ref, out_ref):
    tokens = ids_col_ref.shape[0]
    vocab, width = embed_ref.shape
    picks = lax.broadcasted_iota(jnp.int32, (tokens, vocab), 1) == ids_col_ref[...]
    picks = jnp.where(picks, 1.0, 0.0).astype(BF16)
    ids = ids_ref[...]
    high = ids // 2
    spare = lax.broadcasted_iota(jnp.int32, (8, tokens), 0)
    coded = jnp.where(spare == 0, high, jnp.where(spare == 1, ids - 2 * high, 0)).astype(F32)
    for block in range(width // LANES):
        lane = slice(block * LANES, (block + 1) * LANES)
        inputs = mm(picks, embed_ref[:, lane])
        inputs_ref[:, lane] = inputs.astype(BF16)
        upstream = grad_ref[:, lane].astype(F32) * inputs
        turned = upstream.T.astype(BF16)
        rows = [weight_ref[8 * g : 8 * g + 8, lane].astype(F32) for g in range(HALVES)]
        for k, piece in enumerate(swap_blocks(rows)):
            peer = block * HALVES + k
            out_ref[peer, 0:SIDE, :] = turned[k * SIDE : (k + 1) * SIDE]
            out_ref[peer, SIDE : SIDE + 16, :] = jnp.concatenate([piece, coded], axis=0).astype(
                BF16
            )


def read_ids(block_ref, peer):
    tail = block_ref[peer, SIDE : SIDE + 16, :].astype(F32)
    return (2.0 * tail[8:9] + tail[9:10]).astype(jnp.int32)


def forward_kernel(
    block_ref, embed_ref, spectrum_ref, exact_ref, twist_ref, mix_ref, unmix_ref, back_ref,
    out_ref, values_ref, weight_ref, table_ref,
):
    peers = block_ref.shape[0]
    vocab = embed_ref.shape[0]

    @pl.loop(0, peers)
    def _(peer):
        part = block_ref[peer, SIDE : SIDE + 16, :].astype(F32)[:8]
        lane = lax.broadcasted_iota(jnp.int32, part.shape, 1) // SIDE
        rows = [jnp.where(lane == g, part, 0.0) for g in range(HALVES)]
        weight_ref[pl.ds(pl.multiple_of(peer * SIDE, SIDE), SIDE), :] = jnp.concatenate(
            rows, axis=0
        ).astype(BF16)

    table = mm(embed_ref[...], weight_ref[...])
    table = table + pltpu.roll(table, 2 * SIDE, 1)
    table = table + pltpu.roll(table, SIDE, 1)
    table_ref[...] = table.T[:SIDE].astype(BF16)

    @pl.loop(0, peers // 2)
    def _(step):
        picks = [one_hot_columns(read_ids(block_ref, 2 * step + k), vocab) for k in range(2)]
        columns = mm(table_ref[...], jnp.concatenate(picks, axis=1)).astype(BF16).astype(F32)
        rows = jnp.concatenate([columns[:, :LANES], columns[:, LANES:]], axis=0)
        values_ref[pl.ds(pl.multiple_of(step * 2 * SIDE, 2 * SIDE), 2 * SIDE), :] = rows

    convolve(values_ref, spectrum_ref, (exact_ref, twist_ref, mix_ref, unmix_ref, back_ref), 1.0)
    out_ref[...] = values_ref[...].astype(BF16).reshape(out_ref.shape)


def backward_kernel(
    block_ref, embed_ref, spectrum_ref, exact_ref, twist_ref, mix_ref, unmix_ref, back_ref,
    out_ref, values_ref, sums_ref,
):
    peers = block_ref.shape[0]
    vocab, width = embed_ref.shape
    scaling = 1.0 / math.sqrt(peers * LANES)

    @pl.loop(0, peers)
    def _(peer):
        values_ref[pl.ds(pl.multiple_of(peer * SIDE, SIDE), SIDE), :] = block_ref[
            peer, 0:SIDE, :
        ].astype(F32)

    convolve(values_ref, spectrum_ref, (exact_ref, twist_ref, mix_ref, unmix_ref, back_ref), -1.0)
    sums_ref[...] = jnp.zeros_like(sums_ref)

    @pl.loop(0, peers // 2)
    def _(step):
        picks = [one_hot_columns(read_ids(block_ref, 2 * step + k), vocab) for k in range(2)]
        rows = values_ref[pl.ds(pl.multiple_of(step * 2 * SIDE, 2 * SIDE), 2 * SIDE), :]
        columns = jnp.concatenate([rows[:SIDE], rows[SIDE:]], axis=1).astype(BF16)
        sums_ref[...] += lax.dot_general(
            columns,
            jnp.concatenate(picks, axis=1),
            (((1,), (1,)), ((), ())),
            preferred_element_type=F32,
        )

    both = jnp.concatenate(halves(sums_ref[...]), axis=0)
    for block in range(width // LANES):
        lane = slice(block * LANES, (block + 1) * LANES)
        grad = mm(both, embed_ref[:, lane])
        grad = (grad[:SIDE] + grad[SIDE:]) * scaling
        shifted = [grad] + [pltpu.roll(grad, LANES - 8 * g, 1) for g in range(1, HALVES)]
        turned = jnp.concatenate(shifted, axis=0).T
        for k in range(HALVES):
            out_ref[block * HALVES + k] = turned[k * SIDE : k * SIDE + 8]


def momentum_kernel(grad_ref, momentum_ref, feedback_ref, updated_ref, residue_ref, quant_ref):
    width = momentum_ref.shape[1]
    for block in range(width // LANES):
        lane = slice(block * LANES, (block + 1) * LANES)
        parts = swap_blocks([grad_ref[block * HALVES + k] for k in range(HALVES)])
        grad = jnp.concatenate(parts, axis=0)
        updated_ref[:, lane] = momentum_keep * momentum_ref[:, lane] + (1.0 - momentum_keep) * grad
    total = updated_ref[...] + feedback_ref[...]
    scale = jnp.mean(jnp.abs(total), axis=1, keepdims=True) + tiny_shift
    quantized = (scale * jnp.clip(total / scale, -1.0, 1.0)).astype(BF16)
    quant_ref[...] = quantized
    residue_ref[...] = total - quantized.astype(F32)


def output_kernel(conv_ref, inputs_ref, out_ref):
    for block in range(out_ref.shape[1] // LANES):
        lane = slice(block * LANES, (block + 1) * LANES)
        rows = [conv_ref[block * HALVES + k].astype(F32) for k in range(HALVES)]
        conv = jnp.concatenate(rows, axis=0).T
        out_ref[:, lane] = (inputs_ref[:, lane].astype(F32) * conv).astype(BF16)


def call(kernel, out_shape, scratch=(), flops=0, moved=0):
    return pl.pallas_call(
        kernel,
        out_shape=out_shape,
        scratch_shapes=list(scratch),
        compiler_params=pltpu.CompilerParams(vmem_limit_bytes=VMEM_LIMIT),
        cost_estimate=pl.CostEstimate(flops=flops, bytes_accessed=moved, transcendentals=0),
    )


def exchange(values):
    return lax.all_to_all(values, "seq", split_axis=0, concat_axis=0, tiled=True)


def per_device(ids, embed, weight, filters, out_grad, momentum, feedback):
    parts = lax.axis_size("seq")
    replicas = lax.axis_size("dp")
    vocab, width = embed.shape
    tokens = ids.shape[1]
    channels = filters.shape[0]
    rows = channels * parts
    shape = jax.ShapeDtypeStruct
    tables = transform_tables(parts, tokens)
    convolve_tables = [tables[name] for name in ("exact", "twist", "mix", "unmix", "back")]

    inputs, block = call(
        send_kernel,
        (shape((tokens, width), BF16), shape((parts, SIDE + 16, tokens), BF16)),
        flops=2 * tokens * vocab * width,
        moved=5 << 20,
    )(ids, ids.reshape(tokens, 1), embed, weight, out_grad[0])
    block = exchange(block)
    spectrum = call(
        spectrum_kernel,
        shape((rows, 2 * tokens), F32),
        flops=5 << 30,
        moved=3 << 20,
    )(filters.reshape(channels, parts, tokens), tables["wide"], tables["twist"], tables["mix"])
    gradient = call(
        backward_kernel,
        shape((parts, 8, tokens), F32),
        [pltpu.VMEM((rows, tokens), F32), pltpu.VMEM((channels, vocab), F32)],
        flops=10 << 30,
        moved=6 << 20,
    )(block, embed, spectrum, *convolve_tables)
    gradient = exchange(gradient)
    convolved = call(
        forward_kernel,
        shape((parts, channels, tokens), BF16),
        [
            pltpu.VMEM((rows, tokens), F32),
            pltpu.VMEM((width, LANES), BF16),
            pltpu.VMEM((channels, vocab), BF16),
        ],
        flops=10 << 30,
        moved=6 << 20,
    )(block, embed, spectrum, *convolve_tables)
    convolved = exchange(convolved)
    updated, residue, quantized = call(
        momentum_kernel,
        (
            shape((weight.shape[0], width), F32),
            shape((weight.shape[0], width), F32),
            shape((weight.shape[0], width), BF16),
        ),
        flops=1 << 20,
        moved=2 << 20,
    )(gradient, momentum[0], feedback[0])
    sums = [quantized.astype(F32)]
    for flip in range(1, replicas):
        moved = lax.ppermute(
            quantized, "dp", [(source, source ^ flip) for source in range(replicas)]
        )
        sums.append(moved.astype(F32))
    while len(sums) > 1:
        sums = [left + right for left, right in zip(sums[0::2], sums[1::2])]
    summed = sums[0]
    new_weight = (weight.astype(F32) - step_rate * (summed / replicas)).astype(BF16)
    output = call(
        output_kernel, shape((tokens, width), BF16), flops=1 << 20, moved=2 << 20
    )(convolved, inputs)
    return (output[None], updated[None], residue[None], new_weight)


def solution(mesh):
    placed = (
        P("dp", "seq"),
        P(),
        P("seq", None),
        P("seq", None),
        P("dp", "seq", None),
        P("dp", "seq", None),
        P("dp", "seq", None),
    )
    return jax.shard_map(
        per_device,
        mesh=mesh,
        in_specs=placed,
        out_specs=(
            P("dp", "seq", None),
            P("dp", "seq", None),
            P("dp", "seq", None),
            P("seq", None),
        ),
        check_vma=False,
    )
```

time: 849 us -> 117 us (0.14); the launches traced: 836 us -> 116 us
  waiting for transfers between devices: 597 us -> 30.6 us
  matrix products: 128 us -> 0 us
  blocking collectives: 50.4 us -> 0 us
  Pallas kernels: 0 us -> 32.2 us
  between operations: 14.6 us -> 0.82 us
  starting transfers between devices: 20.7 us -> 33.3 us
    reduce_scatter x1 -> x0, waiting for transfers between devices: 302 us -> none  [per_device(): lax.psum_scatter(jnp.dot(columns.T, downstream, preferred_element_type=jn...]
    all_gather x1 -> x0, waiting for transfers between devices: 255 us -> none  [per_device(): lax.all_gather(weight, 'seq', axis=0, tiled=True)]
    dot_general x33 -> x0, matrix products: 128 us -> none  [the longest x3 20.5 us: forward_transform(): jnp.einsum('ca,jab->jcb', first_imag, grid, precision=lax.Precision.HIGHEST)]
    all_to_all x2 -> x0, blocking collectives: 50.4 us -> none  [the longest x1 25.7 us: per_device(): lax.all_to_all(back_cols, 'seq', split_axis=0, concat_axis=1, tiled=True)]
    psum x1 -> x0, waiting for transfers between devices: 38.6 us -> none  [per_device(): lax.psum(quantized.astype(jnp.float32).astype(jnp.bfloat16), 'dp')]
    pallas_call x0 -> x6, Pallas kernels: none -> 32.2 us  [the longest x1 13.7 us: per_device(): call(backward_kernel, shape((parts, 8, tokens), F32), [pltpu.VMEM((rows,...]
    all_to_all x2 -> x3, waiting for transfers between devices: 0.01 us -> 23.7 us  [exchange(): lax.all_to_all(values, 'seq', split_axis=0, concat_axis=0, tiled=True)]
    all_to_all x2 -> x3, starting transfers between devices: 20.6 us -> 29.9 us  [exchange(): lax.all_to_all(values, 'seq', split_axis=0, concat_axis=0, tiled=True)]
  transfers between devices with their start and end apart: 5 -> 6, of which waited for: 3 -> 4; matrix products, arithmetic and copies ran while one was open for 11% -> 1% of each run, Pallas kernels for 0% -> 13%
where the time goes in v1:
time: 117 us; the launch traced here: 116 us
  starting transfers between devices  33.3 us (28%)
  Pallas kernels  32.2 us (28%)
  waiting for transfers between devices  30.6 us (26%)
  local copies, waits for them, and re-layouts  18.2 us (16%)
    all_to_all x3, starting transfers between devices, exchange(): lax.all_to_all(values, 'seq', split_axis=0, concat_axis=0, tiled=True)  29.9 us
    all_to_all x3, waiting for transfers between devices, exchange(): lax.all_to_all(values, 'seq', split_axis=0, concat_axis=0, tiled=True)  23.7 us
    unnamed x53, local copies, waits for them, and re-layouts  17.4 us
    pallas_call x1, Pallas kernels, per_device(): call(backward_kernel, shape((parts, 8, tokens), F32), [pltpu.VMEM((rows,...  13.7 us
    pallas_call x1, Pallas kernels, per_device(): call(forward_kernel, shape((parts, channels, tokens), BF16), [pltpu.VMEM(...  12.3 us
    ppermute x3, waiting for transfers between devices, per_device(): lax.ppermute(quantized, 'dp', [(source, source ^ flip) for source in rang...  6.9 us
    ppermute x3, starting transfers between devices, per_device(): lax.ppermute(quantized, 'dp', [(source, source ^ flip) for source in rang...  3.37 us
  transfers between devices with their start and end apart: 6, of which 4 were waited for; matrix products, arithmetic and copies ran while one was open for 1% of the time, Pallas kernels for 13%

profile of v1, /device:TPU:6, one launch (start us, length us, event | category | flops | bytes accessed | tf_op | source)
XLA Modules:
  0.0 115.8 jit_solution(531219393042876692)
XLA Ops:
  1.4 1.6 %copy-done = bf16[512,2048]{1,0:T(8,128)(2,1)S(1)} copy-done((bf16[512,2048]{1,0:T(8,128)(2,1)S(1)}, bf16[512,2048]{1,0:T(8,128)(2,1)}, u32[]{:S(2)}) %copy-start) | copy-done | bytes 2097176
  3.0 0.9 copy-done.5
  3.9 1.0 copy-done.7
  5.6 1.8 %shard_map.156 = (bf16[128,2048]{1,0:T(8,128)(2,1)S(1)}, bf16[64,48,128]{2,1,0:T(8,128)(2,1)}) custom-call(s32[1,128]{1,0:T(1,128)S(1)} %copy-done.11, s32[128,1]{1,0:T(8,128)S(1)} %copy.17.ids_col_ref, bf16[512,2048]{1,0:T(8,128)(2,1)S(1)} %copy-done, bf16[32,2048]{1,0:T(8,128)(2,1)S(1)} %copy-done.5, bf16[128,2048]{1,0:T(8,128)(2,1)S(1)} %bitcast.10), custom_call_target="tpu_custom_call" | custom-call | flops 268435456 | bytes 5242880 | tf_op jit(solution)/shard_map/pallas_call | solution.py:334
  8.2 13.3 %all-to-all-start = ((bf16[64,48,128]{2,1,0:T(8,128)(2,1)}), bf16[64,48,128]{2,1,0:T(8,128)(2,1)S(1)}, u32[]{:S(2)}, u32[]{:S(2)}) async-start(bf16[64,48,128]{2,1,0:T(8,128)(2,1)} %get-tuple-element.9), calls=%async_computation | async-start | bytes 1572864 | tf_op jit(solution)/shard_map/all_to_all | solution.py:320
  21.9 2.2 %shard_map.157.spectrum_ref = f32[2048,256]{1,0:T(8,128)S(1)} custom-call(f32[32,64,128]{2,1,0:T(8,128)S(1)} %bitcast.9, bf16[128,192]{1,0:T(8,128)(2,1)S(1)} %copy-done.17, f32[64,256]{1,0:T(8,128)S(1)} %copy-done.15, bf16[2,256,256]{2,1,0:T(8,128)(2,1)S(1)} %copy-done.12), custom_call_target="tpu_custom_call" | custom-call | flops 5368709120 | bytes 3145728 | tf_op jit(solution)/shard_map/pallas_call | solution.py:341
  24.0 1.3 %copy-done.22 = f32[2048,256]{1,0:T(8,128)} copy-done((f32[2048,256]{1,0:T(8,128)}, f32[2048,256]{1,0:T(8,128)S(1)}, u32[]{:S(2)}) %copy-start.22) | copy-done | bytes 2097176
  25.4 20.4 %all-to-all-done.block_ref = bf16[64,48,128]{2,1,0:T(8,128)(2,1)S(1)} async-done(((bf16[64,48,128]{2,1,0:T(8,128)(2,1)}), bf16[64,48,128]{2,1,0:T(8,128)(2,1)S(1)}, u32[]{:S(2)}, u32[]{:S(2)}) %all-to-all-start) | async-done | bytes 786464 | tf_op jit(solution)/shard_map/all_to_all | solution.py:320
  45.8 0.9 copy-done.13
  46.7 1.6 %copy-done.23 = f32[2048,256]{1,0:T(8,128)S(1)} copy-done((f32[2048,256]{1,0:T(8,128)S(1)}, f32[2048,256]{1,0:T(8,128)}, u32[]{:S(2)}) %copy-start.23) | copy-done | bytes 2097176
  48.3 13.7 %shard_map.160 = f32[64,8,128]{2,1,0:T(8,128)S(1)} custom-call(bf16[64,48,128]{2,1,0:T(8,128)(2,1)S(1)} %all-to-all-done.block_ref, bf16[512,2048]{1,0:T(8,128)(2,1)S(1)} %copy-done.1, f32[2048,256]{1,0:T(8,128)S(1)} %copy-done.23, bf16[128,128]{1,0:T(8,128)(2,1)S(1)} %copy-done.20, f32[64,256]{1,0:T(8,128)S(1)} %copy-done.15, ...), custom_call_target="tpu_custom_call" | custom-call | flops 10737418240 | bytes 6291456 | tf_op jit(solution)/shard_map/pallas_call | solution.py:347
  62.8 5.1 %all-to-all-start.2 = ((f32[64,8,128]{2,1,0:T(8,128)}), f32[64,8,128]{2,1,0:T(8,128)S(1)}, u32[]{:S(2)}, u32[]{:S(2)}) async-start(f32[64,8,128]{2,1,0:T(8,128)} %copy-done.10), calls=%async_computation.2 | async-start | bytes 524288 | tf_op jit(solution)/shard_map/all_to_all | solution.py:320
  68.0 0.9 copy-done.14
  71.3 1.6 %copy-done.24 = f32[2048,256]{1,0:T(8,128)S(1)} copy-done((f32[2048,256]{1,0:T(8,128)S(1)}, f32[2048,256]{1,0:T(8,128)}, u32[]{:S(2)}) %copy-start.24) | copy-done | bytes 2097176
  72.9 12.3 %shard_map.158 = bf16[64,32,128]{2,1,0:T(8,128)(2,1)S(1)} custom-call(bf16[64,48,128]{2,1,0:T(8,128)(2,1)S(1)} %all-to-all-done.block_ref, bf16[512,2048]{1,0:T(8,128)(2,1)S(1)} %copy-done.1, f32[2048,256]{1,0:T(8,128)S(1)} %copy-done.24, bf16[128,128]{1,0:T(8,128)(2,1)S(1)} %copy-done.21, f32[64,256]{1,0:T(8,128)S(1)} %copy-done.16, ...), custom_call_target="tpu_custom_call" | custom-call | flops 10737418240 | bytes 6291456 | tf_op jit(solution)/shard_map/pallas_call | solution.py:355
  86.0 11.4 %all-to-all-start.1 = ((bf16[64,32,128]{2,1,0:T(8,128)(2,1)}), bf16[64,32,128]{2,1,0:T(8,128)(2,1)S(1)}, u32[]{:S(2)}, u32[]{:S(2)}) async-start(bf16[64,32,128]{2,1,0:T(8,128)(2,1)} %copy-done.4), calls=%async_computation.1 | async-start | bytes 1048576 | tf_op jit(solution)/shard_map/all_to_all | solution.py:320
  97.5 0.9 copy-done.8
  98.4 0.9 copy-done.9
  99.4 1.1 shard_map.161
  100.5 1.4 %collective-permute-start.1 = (bf16[32,2048]{1,0:T(8,128)(2,1)S(1)}, bf16[32,2048]{1,0:T(8,128)(2,1)S(1)}, u32[]{:S(2)}, u32[]{:S(2)}) collective-permute-start(bf16[32,2048]{1,0:T(8,128)(2,1)S(1)} %get-tuple-element.13), channel_id=1, source_target_pairs={{0,128},{64,192},{128,0},{192,64},{1,129},{65,193},{129,1},{193,65... | collective-permute-start | bytes 393224 | tf_op jit(solution)/shard_map/ppermute | solution.py:379
  101.9 1.9 %collective-permute-start = (bf16[32,2048]{1,0:T(8,128)(2,1)S(1)}, bf16[32,2048]{1,0:T(8,128)(2,1)S(1)}, u32[]{:S(2)}, u32[]{:S(2)}) collective-permute-start(bf16[32,2048]{1,0:T(8,128)(2,1)S(1)} %get-tuple-element.13), channel_id=1, source_target_pairs={{0,64},{64,0},{128,192},{192,128},{1,65},{65,1},{129,193},{193,129... | collective-permute-start | bytes 393224 | tf_op jit(solution)/shard_map/ppermute | solution.py:379
  103.8 6.2 %collective-permute-done.2 = bf16[32,2048]{1,0:T(8,128)(2,1)S(1)} collective-permute-done((bf16[32,2048]{1,0:T(8,128)(2,1)S(1)}, bf16[32,2048]{1,0:T(8,128)(2,1)S(1)}, u32[]{:S(2)}, u32[]{:S(2)}) %collective-permute-start.2) | collective-permute-done | bytes 131104 | tf_op jit(solution)/shard_map/ppermute | solution.py:379
  111.5 3.3 %all-to-all-done.1.conv_ref = bf16[64,32,128]{2,1,0:T(8,128)(2,1)S(1)} async-done(((bf16[64,32,128]{2,1,0:T(8,128)(2,1)}), bf16[64,32,128]{2,1,0:T(8,128)(2,1)S(1)}, u32[]{:S(2)}, u32[]{:S(2)}) %all-to-all-start.1) | async-done | bytes 524320 | tf_op jit(solution)/shard_map/all_to_all | solution.py:320
  114.8 1.0 shard_map.159
  (49 shorter events, 7.8 us)
Async XLA Ops:
  1.4 1.6 %copy-start = (bf16[512,2048]{1,0:T(8,128)(2,1)S(1)}, bf16[512,2048]{1,0:T(8,128)(2,1)}, u32[]{:S(2)}) copy-start(bf16[512,2048]{1,0:T(8,128)(2,1)} %embed_ref.5) | copy-start | bytes 6291460
  3.9 1.0 copy-start.7
  5.6 16.0 %copy-start.25 = (f32[32,8192]{1,0:T(8,128)S(1)}, f32[32,8192]{1,0:T(8,128)}, u32[]{:S(2)}) copy-start(f32[32,8192]{1,0:T(8,128)} %param.16) | copy-start | bytes 3145732
  8.2 13.6 %copy-start.12 = (bf16[2,256,256]{2,1,0:T(8,128)(2,1)S(1)}, bf16[2,256,256]{2,1,0:T(8,128)(2,1)}, u32[]{:S(2)}) copy-start(bf16[2,256,256]{2,1,0:T(8,128)(2,1)} %constant.19.clone.mix_ref) | copy-start | bytes 786436
  8.2 13.6 %copy-start.15 = (f32[64,256]{1,0:T(8,128)S(1)}, f32[64,256]{1,0:T(8,128)}, u32[]{:S(2)}) copy-start(f32[64,256]{1,0:T(8,128)} %constant.18.clone.twist_ref) | copy-start | bytes 196612
  8.2 13.6 %copy-start.17 = (bf16[128,192]{1,0:T(8,128)(2,1)S(1)}, bf16[128,192]{1,0:T(8,128)(2,1)}, u32[]{:S(2)}) copy-start(bf16[128,192]{1,0:T(8,128)(2,1)} %constant.17.clone.wide_ref) | copy-start | bytes 147460
  8.2 37.6 %all-to-all-start = ((bf16[64,48,128]{2,1,0:T(8,128)(2,1)}), bf16[64,48,128]{2,1,0:T(8,128)(2,1)S(1)}, u32[]{:S(2)}, u32[]{:S(2)}) async-start(bf16[64,48,128]{2,1,0:T(8,128)(2,1)} %get-tuple-element.9), calls=%async_computation | async-start | bytes 1572864 | tf_op jit(solution)/shard_map/all_to_all | solution.py:320
  21.8 24.0 %copy-start.1 = (bf16[512,2048]{1,0:T(8,128)(2,1)S(1)}, bf16[512,2048]{1,0:T(8,128)(2,1)}, u32[]{:S(2)}) copy-start(bf16[512,2048]{1,0:T(8,128)(2,1)} %embed_ref.5) | copy-start | bytes 6291460
  21.8 24.0 %copy-start.18 = (bf16[64,384]{1,0:T(8,128)(2,1)S(1)}, bf16[64,384]{1,0:T(8,128)(2,1)}, u32[]{:S(2)}) copy-start(bf16[64,384]{1,0:T(8,128)(2,1)} %constant.22.clone.back_ref) | copy-start | bytes 147460
  21.8 24.0 %copy-start.20 = (bf16[128,128]{1,0:T(8,128)(2,1)S(1)}, bf16[128,128]{1,0:T(8,128)(2,1)}, u32[]{:S(2)}) copy-start(bf16[128,128]{1,0:T(8,128)(2,1)} %constant.20.clone.exact_ref) | copy-start | bytes 98308
  24.0 1.3 %copy-start.22 = (f32[2048,256]{1,0:T(8,128)}, f32[2048,256]{1,0:T(8,128)S(1)}, u32[]{:S(2)}) copy-start(f32[2048,256]{1,0:T(8,128)S(1)} %shard_map.157.spectrum_ref) | copy-start | bytes 6291460
  45.8 1.0 copy-start.13
  46.7 1.6 %copy-start.23 = (f32[2048,256]{1,0:T(8,128)S(1)}, f32[2048,256]{1,0:T(8,128)}, u32[]{:S(2)}) copy-start(f32[2048,256]{1,0:T(8,128)} %copy-done.22) | copy-start | bytes 6291460
  62.8 23.2 %all-to-all-start.2 = ((f32[64,8,128]{2,1,0:T(8,128)}), f32[64,8,128]{2,1,0:T(8,128)S(1)}, u32[]{:S(2)}, u32[]{:S(2)}) async-start(f32[64,8,128]{2,1,0:T(8,128)} %copy-done.10), calls=%async_computation.2 | async-start | bytes 524288 | tf_op jit(solution)/shard_map/all_to_all | solution.py:320
  68.0 1.0 copy-start.14
  71.3 1.6 %copy-start.24 = (f32[2048,256]{1,0:T(8,128)S(1)}, f32[2048,256]{1,0:T(8,128)}, u32[]{:S(2)}) copy-start(f32[2048,256]{1,0:T(8,128)} %copy-done.22) | copy-start | bytes 6291460
  72.9 37.8 %copy-start.6 = (bf16[32,2048]{1,0:T(8,128)(2,1)S(1)}, bf16[32,2048]{1,0:T(8,128)(2,1)}, u32[]{:S(2)}) copy-start(bf16[32,2048]{1,0:T(8,128)(2,1)} %weight_ref.1) | copy-start | bytes 393220
  86.0 28.8 %copy-start.3 = (bf16[128,2048]{1,0:T(8,128)(2,1)S(1)}, bf16[128,2048]{1,0:T(8,128)(2,1)}, u32[]{:S(2)}) copy-start(bf16[128,2048]{1,0:T(8,128)(2,1)} %copy-done.2) | copy-start | bytes 1572868
  86.0 28.8 %all-to-all-start.1 = ((bf16[64,32,128]{2,1,0:T(8,128)(2,1)}), bf16[64,32,128]{2,1,0:T(8,128)(2,1)S(1)}, u32[]{:S(2)}, u32[]{:S(2)}) async-start(bf16[64,32,128]{2,1,0:T(8,128)(2,1)} %copy-done.4), calls=%async_computation.1 | async-start | bytes 1048576 | tf_op jit(solution)/shard_map/all_to_all | solution.py:320
  97.5 1.0 copy-start.8
  98.4 0.9 copy-start.9
  100.5 9.6 %collective-permute-start.2 = (bf16[32,2048]{1,0:T(8,128)(2,1)S(1)}, bf16[32,2048]{1,0:T(8,128)(2,1)S(1)}, u32[]{:S(2)}, u32[]{:S(2)}) collective-permute-start(bf16[32,2048]{1,0:T(8,128)(2,1)S(1)} %get-tuple-element.13), channel_id=1, source_target_pairs={{0,192},{64,128},{128,64},{192,0},{1,193},{65,129},{129,65},{193,1... | collective-permute-start | bytes 393224 | tf_op jit(solution)/shard_map/ppermute | solution.py:379
  100.5 10.3 %collective-permute-start.1 = (bf16[32,2048]{1,0:T(8,128)(2,1)S(1)}, bf16[32,2048]{1,0:T(8,128)(2,1)S(1)}, u32[]{:S(2)}, u32[]{:S(2)}) collective-permute-start(bf16[32,2048]{1,0:T(8,128)(2,1)S(1)} %get-tuple-element.13), channel_id=1, source_target_pairs={{0,128},{64,192},{128,0},{192,64},{1,129},{65,193},{129,1},{193,65... | collective-permute-start | bytes 393224 | tf_op jit(solution)/shard_map/ppermute | solution.py:379
  101.9 8.8 %collective-permute-start = (bf16[32,2048]{1,0:T(8,128)(2,1)S(1)}, bf16[32,2048]{1,0:T(8,128)(2,1)S(1)}, u32[]{:S(2)}, u32[]{:S(2)}) collective-permute-start(bf16[32,2048]{1,0:T(8,128)(2,1)S(1)} %get-tuple-element.13), channel_id=1, source_target_pairs={{0,64},{64,0},{128,192},{192,128},{1,65},{65,1},{129,193},{193,129... | collective-permute-start | bytes 393224 | tf_op jit(solution)/shard_map/ppermute | solution.py:379
  (8 other events, 6.3 us)

commit v2 on v1

v2 whole, which is shorter than its diff:
```python
import functools
import math

import jax
import jax.numpy as jnp
import numpy as np
from jax import lax
from jax.experimental import pallas as pl
from jax.experimental.pallas import tpu as pltpu
from jax.sharding import PartitionSpec as P

momentum_keep = 0.9
step_rate = 0.02
tiny_shift = 1e-06

F32 = jnp.float32
BF16 = jnp.bfloat16
LANES = 128
GROUP = 16
STEP = 8
TAIL = 8
SENT = 6
HALVES = 4
SIDE = 32
VMEM_LIMIT = 58 * 1024 * 1024
CHUNKS = 2
TABLES = 4


def split_const(table):
    high = np.asarray(table, np.float32).astype(BF16)
    low = (table - high.astype(np.float64)).astype(np.float32).astype(BF16)
    return high, low


def transform_tables(outer, inner):
    total = outer * inner
    freq = np.arange(outer)[:, None] + 0.25
    first = np.exp(-2j * np.pi * freq * np.arange(outer)[None, :] / outer)
    twist = np.exp(-2j * np.pi * freq * np.arange(inner)[None, :] / total)
    second = np.exp(
        -2j * np.pi * (np.arange(inner)[:, None] * np.arange(inner)[None, :] % inner) / inner
    )
    stage = np.concatenate([first.real, first.imag], axis=0)
    high, low = split_const(stage)
    back_high, back_low = split_const(stage.T)
    real, imag = second.real, second.imag
    mix = np.block([[real, imag], [-imag, real]])
    return {
        "exact": np.concatenate([high, low], axis=1),
        "wide": np.concatenate([high, high, low], axis=1),
        "back": np.concatenate([back_high, back_high, back_low], axis=1),
        "twist": np.concatenate([twist.real, twist.imag], axis=1).astype(np.float32),
        "mix": np.stack(split_const(mix)),
    }


def mm(left, right):
    return jnp.dot(left, right, preferred_element_type=F32)


def halves(values):
    high = values.astype(BF16)
    return high, (values - high.astype(F32)).astype(BF16)


def mm_wide(values, table_ref):
    rows = values.shape[0]
    high, low = halves(values)
    both = mm(jnp.concatenate([high, low], axis=0), table_ref[0])
    return both[:rows] + both[rows:] + mm(high, table_ref[1])


def spread(columns, stage_ref, twist_ref, exact):
    real_twist = twist_ref[:, :LANES]
    imag_twist = twist_ref[:, LANES:]
    outer = real_twist.shape[0]
    rows = []
    for first in range(0, len(columns), 2):
        pair = jnp.concatenate(columns[first : first + 2], axis=1)
        if exact:
            high = pair.astype(BF16)
            stack = jnp.concatenate([high, high], axis=0)
        else:
            high, low = halves(pair)
            stack = jnp.concatenate([high, low, high], axis=0)
        grid = mm(stage_ref[...], stack)
        for which in range(2):
            lane = slice(which * LANES, (which + 1) * LANES)
            real = grid[:outer, lane]
            imag = grid[outer:, lane]
            rows.append(
                jnp.concatenate(
                    [
                        real * real_twist - imag * imag_twist,
                        real * imag_twist + imag * real_twist,
                    ],
                    axis=1,
                )
            )
    return jnp.concatenate(rows, axis=0)


def gather_back(spectrum, back_ref, twist_ref):
    real_twist = twist_ref[:, :LANES]
    imag_twist = twist_ref[:, LANES:]
    outer = real_twist.shape[0]
    count = spectrum.shape[0] // outer
    turned = []
    for which in range(count):
        real = spectrum[which * outer : (which + 1) * outer, :LANES]
        imag = spectrum[which * outer : (which + 1) * outer, LANES:]
        turned.append(
            jnp.concatenate(
                [
                    real * real_twist - imag * imag_twist,
                    -(imag * real_twist + real * imag_twist),
                ],
                axis=0,
            )
        )
    columns = []
    for first in range(0, count, 2):
        high, low = halves(jnp.concatenate(turned[first : first + 2], axis=1))
        pair = mm(back_ref[...], jnp.concatenate([high, low, high], axis=0))
        columns += [pair[:, :LANES], pair[:, LANES:]]
    return columns


def start_all(pairs, sems, first=0):
    copies = [
        pltpu.make_async_copy(source, target, sems.at[first + which])
        for which, (source, target) in enumerate(pairs)
    ]
    for copy in copies:
        copy.start()
    return copies


def wait_all(copies):
    for copy in copies:
        copy.wait()


def group_rows(which, outer):
    return pl.ds(which * GROUP * outer, GROUP * outer)


def token_picks(ids, vocab):
    column = jnp.broadcast_to(ids.astype(F32), (LANES, ids.shape[1])).T
    lane_index = lax.broadcasted_iota(jnp.int32, column.shape, 1).astype(F32)
    return jnp.concatenate(
        [
            jnp.where(column == lane_index + first, 1.0, 0.0).astype(BF16)
            for first in range(0, vocab, LANES)
        ],
        axis=1,
    )


def spectrum_kernel(
    filters_ref, wide_ref, twist_ref, mix_ref, ids_ref, embed_ref,
    out_hbm, inputs_ref, values_ref, out_ref, sems,
):
    channels, length = filters_ref.shape
    outer = length // LANES
    norm = 1.0 / length
    for block in range(outer):
        values_ref[block * channels : (block + 1) * channels, :] = (
            filters_ref[:, block * LANES : (block + 1) * LANES] * norm
        )
    copies = []
    for which in range(channels // GROUP):
        columns = [
            values_ref[pl.ds(which * GROUP + k, outer, stride=channels), :] for k in range(GROUP)
        ]
        bins = group_rows(which, outer)
        out_ref[bins, :] = mm_wide(spread(columns, wide_ref, twist_ref, False), mix_ref)
        copies += start_all([(out_ref.at[bins], out_hbm.at[bins])], sems, which)
    inputs_ref[...] = mm(token_picks(ids_ref[...], embed_ref.shape[0]), embed_ref[...]).astype(
        BF16
    )
    wait_all(copies)


def convolve(values_ref, spectrum_ref, tables, sign, arrivals):
    exact_ref, twist_ref, mix_ref, back_ref = tables
    outer = twist_ref.shape[0]
    channels = values_ref.shape[0] // outer
    for which in range(channels // GROUP):
        base = which * GROUP
        columns = [
            values_ref[pl.ds(base + k, outer, stride=channels), :] for k in range(GROUP)
        ]
        bins = mm_wide(spread(columns, exact_ref, twist_ref, True), mix_ref)
        arrivals[which].wait()
        filt = spectrum_ref[group_rows(which, outer), :]
        real, imag = bins[:, :LANES], bins[:, LANES:]
        filt_real, filt_imag = filt[:, :LANES], filt[:, LANES:]
        product = jnp.concatenate(
            [
                real * filt_real - sign * (imag * filt_imag),
                -(imag * filt_real + sign * (real * filt_imag)),
            ],
            axis=1,
        )
        result = gather_back(mm_wide(product, mix_ref), back_ref, twist_ref)
        for k in range(GROUP):
            values_ref[pl.ds(base + k, outer, stride=channels), :] = result[k]


def swap_blocks(parts):
    lane = lax.broadcasted_iota(jnp.int32, parts[0].shape, 1) // SIDE
    out = []
    for to in range(HALVES):
        total = None
        for source in range(HALVES):
            moved = parts[source]
            if source != to:
                moved = pltpu.roll(moved, ((source - to) * SIDE) % LANES, 1)
            total = moved if total is None else jnp.where(lane == source, moved, total)
        out.append(total)
    return out


def lane_span(chunk, width):
    span = width // CHUNKS
    return pl.ds(chunk * span, span)


def peer_span(chunk, peers):
    span = peers // CHUNKS
    return pl.ds(chunk * span, span)


def second_core():
    return lax.axis_index("dp") % 2 == 1


def send_kernel(
    ids_ref, embed_hbm, grad_hbm, weight_hbm, out_hbm,
    embed_ref, grad_ref, weight_ref, out_ref, sems,
):
    vocab, width = embed_hbm.shape
    tokens = ids_ref.shape[1]
    peers = out_ref.shape[0]
    copies = start_all([(weight_hbm, weight_ref), (grad_hbm, grad_ref)], sems, 2 * CHUNKS)
    for chunk in range(CHUNKS):
        lane = lane_span(chunk, width)
        copies += start_all([(embed_hbm.at[:, lane], embed_ref.at[:, lane])], sems, chunk)
    ids = ids_ref[...]
    high = ids // LANES
    spare = lax.broadcasted_iota(jnp.int32, (TAIL - SENT, tokens), 0)
    coded = jnp.where(spare == 0, high, ids - LANES * high).astype(F32)
    picks = token_picks(ids, vocab)
    late = second_core()
    sent = []
    wait_all(copies[:2])
    for chunk in range(CHUNKS):
        copies[2 + chunk].wait()
        blocks = width // LANES // CHUNKS
        for block in range(chunk * blocks, (chunk + 1) * blocks):
            lane = slice(block * LANES, (block + 1) * LANES)
            inputs = mm(picks, embed_ref[:, lane]).astype(BF16).astype(F32)
            turned = (grad_ref[:, lane].astype(F32) * inputs).T
            part = weight_ref[:, lane].astype(F32)
            parts = swap_blocks([part[8 * g : 8 * g + 8] for g in range(HALVES)])
            for k, piece in enumerate(parts):
                rows = [
                    turned[k * SIDE : (k + 1) * SIDE],
                    piece[:4],
                    jnp.where(late, piece[6:8], piece[4:6]),
                    coded,
                ]
                out_ref[block * HALVES + k] = jnp.concatenate(rows, axis=0).astype(BF16)
        rows = peer_span(chunk, peers)
        sent += start_all([(out_ref.at[rows], out_hbm.at[rows])], sems, CHUNKS + chunk)
    wait_all(sent)


def read_ids(block_ref, first):
    tails = [block_ref[first + k].astype(F32)[SIDE + SENT :] for k in range(2)]
    both = jnp.concatenate(tails, axis=1)
    high, low = both[0:1], both[1:2]
    index = lax.broadcasted_iota(jnp.int32, (LANES, 2 * LANES), 0).astype(F32)
    return high, jnp.where(index == low, 1.0, 0.0).astype(BF16)


def forward_kernel(
    block_hbm, other_hbm, embed_hbm, spectrum_hbm, exact_hbm, twist_hbm, mix_hbm, back_hbm,
    out_hbm,
    block_ref, other_ref, embed_ref, spectrum_ref, exact_ref, twist_ref, mix_ref, back_ref,
    values_ref, weight_ref, table_ref, out_ref, sems,
):
    peers = block_ref.shape[0]
    vocab, width = embed_ref.shape
    groups = SIDE // GROUP
    half = width // 2
    block_copy, other_copy, embed_first, embed_second = start_all(
        [
            (block_hbm, block_ref),
            (other_hbm, other_ref),
            (embed_hbm.at[:, pl.ds(0, half)], embed_ref.at[:, pl.ds(0, half)]),
            (embed_hbm.at[:, pl.ds(half, half)], embed_ref.at[:, pl.ds(half, half)]),
        ],
        sems,
    )
    table_copies = start_all(
        [
            (exact_hbm, exact_ref),
            (twist_hbm, twist_ref),
            (mix_hbm, mix_ref),
            (back_hbm, back_ref),
        ],
        sems,
        4,
    )
    spectrum_copies = start_all(
        [
            (spectrum_hbm.at[group_rows(k, peers)], spectrum_ref.at[group_rows(k, peers)])
            for k in range(groups)
        ],
        sems,
        4 + TABLES,
    )
    block_copy.wait()
    other_copy.wait()
    late = second_core()

    @pl.loop(0, peers // STEP)
    def _(step):
        others = other_ref[pl.ds(pl.multiple_of(step * 2 * STEP, 2 * STEP), 2 * STEP), :]
        others = others.astype(F32)
        for k in range(STEP):
            peer = step * STEP + k
            tail = block_ref[peer].astype(F32)[SIDE : SIDE + SENT]
            mine, other = tail[4:], others[2 * k : 2 * k + 2]
            part = jnp.concatenate(
                [tail[:4], jnp.where(late, other, mine), jnp.where(late, mine, other)], axis=0
            )
            lane = lax.broadcasted_iota(jnp.int32, part.shape, 1) // SIDE
            rows = [jnp.where(lane == g, part, 0.0) for g in range(HALVES)]
            weight_ref[pl.ds(pl.multiple_of(peer * SIDE, SIDE), SIDE), :] = jnp.concatenate(
                rows, axis=0
            ).astype(BF16)

    embed_first.wait()
    table = mm(embed_ref[:, :half], weight_ref[:half])
    embed_second.wait()
    table = table + mm(embed_ref[:, half:], weight_ref[half:])
    table = table + pltpu.roll(table, 2 * SIDE, 1)
    table = table + pltpu.roll(table, SIDE, 1)
    parts = []
    for part in range(vocab // LANES):
        turned = table[part * LANES : (part + 1) * LANES].T
        parts.append(turned[:SIDE])
    table_ref[...] = jnp.concatenate(parts, axis=0).astype(BF16)

    @pl.loop(0, peers // STEP)
    def _(step):
        for k in range(0, STEP, 2):
            first = step * STEP + k
            high, picks = read_ids(block_ref, first)
            every = mm(table_ref[...], picks)
            columns = every[:SIDE]
            for part in range(1, vocab // LANES):
                columns = jnp.where(
                    high == part, every[part * SIDE : (part + 1) * SIDE], columns
                )
            rows = jnp.concatenate([columns[:, :LANES], columns[:, LANES:]], axis=0)
            values_ref[pl.ds(pl.multiple_of(first * SIDE, 2 * SIDE), 2 * SIDE), :] = rows

    wait_all(table_copies)
    convolve(
        values_ref, spectrum_ref, (exact_ref, twist_ref, mix_ref, back_ref), 1.0, spectrum_copies
    )
    span = peers // CHUNKS
    copies = []
    for chunk in range(CHUNKS):
        rows = pl.ds(chunk * span, span)
        out_ref[rows] = (
            values_ref[pl.ds(chunk * span * SIDE, span * SIDE), :]
            .astype(BF16)
            .reshape(span, SIDE, LANES)
        )
        copies += start_all([(out_ref.at[rows], out_hbm.at[rows])], sems, 4 + TABLES + groups + chunk)
    wait_all(copies)


def backward_kernel(
    block_hbm, embed_hbm, spectrum_hbm, exact_hbm, twist_hbm, mix_hbm, back_hbm,
    out_hbm, other_hbm,
    block_ref, embed_ref, spectrum_ref, exact_ref, twist_ref, mix_ref, back_ref,
    values_ref, sums_ref, out_ref, other_ref, sems,
):
    peers = block_ref.shape[0]
    vocab, width = embed_ref.shape
    groups = SIDE // GROUP
    scaling = 1.0 / math.sqrt(peers * LANES)
    block_copies = start_all(
        [
            (block_hbm, block_ref),
            (exact_hbm, exact_ref),
            (twist_hbm, twist_ref),
            (mix_hbm, mix_ref),
            (back_hbm, back_ref),
        ],
        sems,
    )
    block_copies[0].wait()
    spectrum_copies = start_all(
        [
            (spectrum_hbm.at[group_rows(k, peers)], spectrum_ref.at[group_rows(k, peers)])
            for k in range(groups)
        ],
        sems,
        1 + TABLES,
    )
    (embed_copy,) = start_all([(embed_hbm, embed_ref)], sems, 1 + TABLES + groups)

    @pl.loop(0, peers // STEP)
    def _(step):
        others = []
        for k in range(STEP):
            peer = step * STEP + k
            part = block_ref[peer].astype(F32)
            values_ref[pl.ds(pl.multiple_of(peer * SIDE, SIDE), SIDE), :] = part[:SIDE]
            others.append(part[SIDE + 4 : SIDE + SENT])
        other_ref[pl.ds(pl.multiple_of(step * 2 * STEP, 2 * STEP), 2 * STEP), :] = (
            jnp.concatenate(others, axis=0).astype(BF16)
        )

    copies = start_all([(other_ref, other_hbm)], sems, 2 + TABLES + groups)
    wait_all(block_copies[1:])
    convolve(
        values_ref, spectrum_ref, (exact_ref, twist_ref, mix_ref, back_ref), -1.0, spectrum_copies
    )
    sums_ref[...] = jnp.zeros_like(sums_ref)

    @pl.loop(0, peers // STEP)
    def _(step):
        total = sums_ref[...]
        for k in range(0, STEP, 2):
            first = step * STEP + k
            high, picks = read_ids(block_ref, first)
            rows = values_ref[pl.ds(pl.multiple_of(first * SIDE, 2 * SIDE), 2 * SIDE), :]
            columns = jnp.concatenate([rows[:SIDE], rows[SIDE:]], axis=1)
            masked = [jnp.where(high == part, columns, 0.0) for part in range(vocab // LANES)]
            total = total + lax.dot_general(
                jnp.concatenate(masked, axis=0).astype(BF16),
                picks,
                (((1,), (1,)), ((), ())),
                preferred_element_type=F32,
            )
        sums_ref[...] = total

    sums = sums_ref[...]
    sums = jnp.concatenate(
        [sums[part * SIDE : (part + 1) * SIDE] for part in range(vocab // LANES)], axis=1
    )
    both = jnp.concatenate(halves(sums), axis=0)
    embed_copy.wait()
    blocks = width // LANES // CHUNKS
    for chunk in range(CHUNKS):
        for first in range(chunk * blocks, (chunk + 1) * blocks, 2):
            pair = mm(both, embed_ref[:, first * LANES : (first + 2) * LANES])
            pair = (pair[:SIDE] + pair[SIDE:]) * scaling
            for block in range(first, first + 2):
                lane = slice((block - first) * LANES, (block - first + 1) * LANES)
                grad = pair[:, lane]
                shifted = [grad] + [pltpu.roll(grad, LANES - 8 * g, 1) for g in range(1, HALVES)]
                turned = jnp.concatenate(shifted, axis=0).T
                for k in range(HALVES):
                    out_ref[block * HALVES + k] = turned[k * SIDE : k * SIDE + 8]
        rows = pl.ds(chunk * blocks * HALVES, blocks * HALVES)
        copies += start_all([(out_ref.at[rows], out_hbm.at[rows])], sems, 3 + TABLES + groups + chunk)
    wait_all(copies)


def momentum_kernel(
    grad_hbm, momentum_hbm, feedback_hbm, updated_hbm, residue_hbm, quant_hbm,
    grad_ref, updated_ref, total_ref, quant_ref, sems,
):
    peers = grad_ref.shape[0]
    width = total_ref.shape[1]
    blocks = width // LANES // CHUNKS
    copies = []
    for chunk in range(CHUNKS):
        lane = lane_span(chunk, width)
        rows = peer_span(chunk, peers)
        pairs = [
            (grad_hbm.at[rows], grad_ref.at[rows]),
            (momentum_hbm.at[:, lane], updated_ref.at[:, lane]),
            (feedback_hbm.at[:, lane], total_ref.at[:, lane]),
        ]
        copies.append(start_all(pairs, sems, 3 * chunk))
    sent = []
    weight = 0.0
    for chunk in range(CHUNKS):
        wait_all(copies[chunk])
        for block in range(chunk * blocks, (chunk + 1) * blocks):
            lane = slice(block * LANES, (block + 1) * LANES)
            parts = swap_blocks([grad_ref[block * HALVES + k] for k in range(HALVES)])
            grad = jnp.concatenate(parts, axis=0)
            updated = momentum_keep * updated_ref[:, lane] + (1.0 - momentum_keep) * grad
            updated_ref[:, lane] = updated
            total = updated + total_ref[:, lane]
            total_ref[:, lane] = total
            weight = weight + jnp.abs(total)
        lane = lane_span(chunk, width)
        sent += start_all(
            [(updated_ref.at[:, lane], updated_hbm.at[:, lane])], sems, 3 * CHUNKS + chunk
        )
    scale = jnp.sum(weight, axis=1, keepdims=True) / width + tiny_shift
    for chunk in range(CHUNKS):
        for block in range(chunk * blocks, (chunk + 1) * blocks):
            lane = slice(block * LANES, (block + 1) * LANES)
            total = total_ref[:, lane]
            quantized = (scale * jnp.clip(total / scale, -1.0, 1.0)).astype(BF16)
            quant_ref[:, lane] = quantized
            total_ref[:, lane] = total - quantized.astype(F32)
        lane = lane_span(chunk, width)
        pairs = [
            (quant_ref.at[:, lane], quant_hbm.at[:, lane]),
            (total_ref.at[:, lane], residue_hbm.at[:, lane]),
        ]
        sent += start_all(pairs, sems, 4 * CHUNKS + 2 * chunk)
    wait_all(sent)


def output_kernel(conv_hbm, inputs_hbm, out_hbm, conv_ref, inputs_ref, out_ref, sems):
    peers = conv_ref.shape[0]
    width = out_ref.shape[1]
    blocks = width // LANES // CHUNKS
    copies = []
    for chunk in range(CHUNKS):
        lane = lane_span(chunk, width)
        rows = peer_span(chunk, peers)
        pairs = [
            (conv_hbm.at[rows], conv_ref.at[rows]),
            (inputs_hbm.at[:, lane], inputs_ref.at[:, lane]),
        ]
        copies.append(start_all(pairs, sems, 2 * chunk))
    sent = []
    for chunk in range(CHUNKS):
        wait_all(copies[chunk])
        for block in range(chunk * blocks, (chunk + 1) * blocks):
            lane = slice(block * LANES, (block + 1) * LANES)
            rows = [conv_ref[block * HALVES + k].astype(F32) for k in range(HALVES)]
            conv = jnp.concatenate(rows, axis=0).T
            out_ref[:, lane] = (inputs_ref[:, lane].astype(F32) * conv).astype(BF16)
        lane = lane_span(chunk, width)
        sent += start_all([(out_ref.at[:, lane], out_hbm.at[:, lane])], sems, 2 * CHUNKS + chunk)
    wait_all(sent)


def spaces(kinds):
    return [
        pl.BlockSpec(memory_space={"h": pltpu.HBM, "a": pl.ANY, "v": pltpu.VMEM}[kind])
        for kind in kinds
    ]


def call(kernel, out_shape, ins, outs, scratch=(), flops=0, moved=0):
    out_specs = spaces(outs)
    return pl.pallas_call(
        kernel,
        out_shape=out_shape,
        in_specs=spaces(ins),
        out_specs=out_specs if len(outs) > 1 else out_specs[0],
        scratch_shapes=list(scratch),
        compiler_params=pltpu.CompilerParams(vmem_limit_bytes=VMEM_LIMIT),
        cost_estimate=pl.CostEstimate(flops=flops, bytes_accessed=moved, transcendentals=0),
    )


def exchange(values):
    return lax.all_to_all(values, "seq", split_axis=0, concat_axis=0, tiled=True)


def per_device(ids, embed, weight, filters, out_grad, momentum, feedback):
    parts = lax.axis_size("seq")
    replicas = lax.axis_size("dp")
    vocab, width = embed.shape
    tokens = ids.shape[1]
    channels = filters.shape[0]
    rows = channels * parts
    shape = jax.ShapeDtypeStruct
    tables = transform_tables(parts, tokens)
    convolve_tables = [tables[name] for name in ("exact", "twist", "mix", "back")]

    table_scratch = [
        pltpu.VMEM(table.shape, F32 if table.dtype == np.float32 else BF16)
        for table in convolve_tables
    ]
    groups = channels // GROUP

    block = call(
        send_kernel,
        shape((parts, SIDE + TAIL, tokens), BF16),
        "vhhh",
        "h",
        [
            pltpu.VMEM((vocab, width), BF16),
            pltpu.VMEM((tokens, width), BF16),
            pltpu.VMEM((weight.shape[0], width), BF16),
            pltpu.VMEM((parts, SIDE + TAIL, tokens), BF16),
            pltpu.SemaphoreType.DMA((2 * CHUNKS + 2,)),
        ],
        flops=2 * tokens * vocab * width,
        moved=5 << 20,
    )(ids, embed, out_grad[0], weight)
    block = exchange(block)
    spectrum, inputs = call(
        spectrum_kernel,
        (shape((rows, 2 * tokens), F32), shape((tokens, width), BF16)),
        "vvvvvv",
        "hv",
        [
            pltpu.VMEM((rows, tokens), F32),
            pltpu.VMEM((rows, 2 * tokens), F32),
            pltpu.SemaphoreType.DMA((groups,)),
        ],
        flops=5 << 30,
        moved=3 << 20,
    )(filters, tables["wide"], tables["twist"], tables["mix"], ids, embed)
    gradient, other = call(
        backward_kernel,
        (shape((parts, 8, tokens), F32), shape((2 * parts, tokens), BF16)),
        "ahhhhhh",
        "hh",
        [
            pltpu.VMEM((parts, SIDE + TAIL, tokens), BF16),
            pltpu.VMEM((vocab, width), BF16),
            pltpu.VMEM((rows, 2 * tokens), F32),
            *table_scratch,
            pltpu.VMEM((rows, tokens), F32),
            pltpu.VMEM((LANES, LANES), F32),
            pltpu.VMEM((parts, 8, tokens), F32),
            pltpu.VMEM((2 * parts, tokens), BF16),
            pltpu.SemaphoreType.DMA((3 + TABLES + groups + CHUNKS,)),
        ],
        flops=10 << 30,
        moved=6 << 20,
    )(block, embed, spectrum, *convolve_tables)
    other = lax.ppermute(other, "dp", [(source, source ^ 1) for source in range(replicas)])
    gradient = exchange(gradient)
    convolved = call(
        forward_kernel,
        shape((parts, channels, tokens), BF16),
        "aahhhhhh",
        "h",
        [
            pltpu.VMEM((parts, SIDE + TAIL, tokens), BF16),
            pltpu.VMEM((2 * parts, tokens), BF16),
            pltpu.VMEM((vocab, width), BF16),
            pltpu.VMEM((rows, 2 * tokens), F32),
            *table_scratch,
            pltpu.VMEM((rows, tokens), F32),
            pltpu.VMEM((width, LANES), BF16),
            pltpu.VMEM((LANES, LANES), BF16),
            pltpu.VMEM((parts, channels, tokens), BF16),
            pltpu.SemaphoreType.DMA((4 + TABLES + groups + CHUNKS,)),
        ],
        flops=10 << 30,
        moved=6 << 20,
    )(block, other, embed, spectrum, *convolve_tables)
    convolved = exchange(convolved)
    updated, residue, quantized = call(
        momentum_kernel,
        (
            shape((weight.shape[0], width), F32),
            shape((weight.shape[0], width), F32),
            shape((weight.shape[0], width), BF16),
        ),
        "ahh",
        "hhh",
        [
            pltpu.VMEM((parts, 8, tokens), F32),
            pltpu.VMEM((weight.shape[0], width), F32),
            pltpu.VMEM((weight.shape[0], width), F32),
            pltpu.VMEM((weight.shape[0], width), BF16),
            pltpu.SemaphoreType.DMA((6 * CHUNKS,)),
        ],
        flops=1 << 20,
        moved=2 << 20,
    )(gradient, momentum[0], feedback[0])
    def swap(values, flip):
        return lax.ppermute(values, "dp", [(source, source ^ flip) for source in range(replicas)])

    across = swap(quantized, 2)
    beside = swap(quantized, 1)
    corner = swap(across, 1)
    summed = (quantized.astype(F32) + beside.astype(F32)) + (
        across.astype(F32) + corner.astype(F32)
    )
    new_weight = (weight.astype(F32) - step_rate * (summed / replicas)).astype(BF16)
    output = call(
        output_kernel,
        shape((tokens, width), BF16),
        "aa",
        "h",
        [
            pltpu.VMEM((parts, channels, tokens), BF16),
            pltpu.VMEM((tokens, width), BF16),
            pltpu.VMEM((tokens, width), BF16),
            pltpu.SemaphoreType.DMA((3 * CHUNKS,)),
        ],
        flops=1 << 20,
        moved=2 << 20,
    )(convolved, inputs)
    return (output[None], updated[None], residue[None], new_weight)


def solution(mesh):
    placed = (
        P("dp", "seq"),
        P(),
        P("seq", None),
        P("seq", None),
        P("dp", "seq", None),
        P("dp", "seq", None),
        P("dp", "seq", None),
    )
    return jax.shard_map(
        per_device,
        mesh=mesh,
        in_specs=placed,
        out_specs=(
            P("dp", "seq", None),
            P("dp", "seq", None),
            P("dp", "seq", None),
            P("seq", None),
        ),
        check_vma=False,
    )
```

time: 117 us -> 100 us (0.85)
  local copies, waits for them, and re-layouts: 18.2 us -> 2.24 us
  starting transfers between devices: 33.3 us -> 28.4 us
  Pallas kernels: 32.2 us -> 34.8 us
    unnamed x53 -> x10, local copies, waits for them, and re-layouts: 17.4 us -> 2.24 us
    all_to_all x3, starting transfers between devices: 29.9 us -> 26.8 us  [exchange(): lax.all_to_all(values, 'seq', split_axis=0, concat_axis=0, tiled=True)]
    ppermute x3 -> x4, waiting for transfers between devices: 6.9 us -> 8.84 us  [the longest x3 8.84 us: swap(): lax.ppermute(values, 'dp', [(source, source ^ flip) for source in range(r...]
    ppermute x3 -> x4, starting transfers between devices: 3.37 us -> 1.6 us  [the longest x3 1.51 us: swap(): lax.ppermute(values, 'dp', [(source, source ^ flip) for source in range(r...]
    pallas_call x5, Pallas kernels: 31.1 us -> 32.4 us  [the longest x1 10.5 us: per_device(): call(forward_kernel, shape((parts, channels, tokens), BF16), 'aahhhhhh',...]
    pallas_call x1, Pallas kernels: 1.12 us -> 2.35 us  [per_device(): call(momentum_kernel, (shape((weight.shape[0], width), F32), shape((weigh...]
  transfers between devices with their start and end apart: 6 -> 7, of which waited for: 4 -> 5; matrix products, arithmetic and copies ran while one was open for 1% -> 2% of each run, Pallas kernels for 13% -> 19%
where the time goes in v2:
time: 100 us; the launch traced here: 99.6 us
  Pallas kernels  34.8 us (35%)
  waiting for transfers between devices  31.7 us (32%)
  starting transfers between devices  28.4 us (28%)
  local copies, waits for them, and re-layouts  2.24 us (2%)
  other arithmetic  1.65 us (2%)
    all_to_all x3, starting transfers between devices, exchange(): lax.all_to_all(values, 'seq', split_axis=0, concat_axis=0, tiled=True)  26.8 us
    all_to_all x3, waiting for transfers between devices, exchange(): lax.all_to_all(values, 'seq', split_axis=0, concat_axis=0, tiled=True)  22.9 us
    pallas_call x1, Pallas kernels, per_device(): call(forward_kernel, shape((parts, channels, tokens), BF16), 'aahhhhhh',...  10.5 us
    pallas_call x1, Pallas kernels, per_device(): call(backward_kernel, (shape((parts, 8, tokens), F32), shape((2 * parts,...  9.93 us
    ppermute x3, waiting for transfers between devices, swap(): lax.ppermute(values, 'dp', [(source, source ^ flip) for source in range(r...  8.84 us
    pallas_call x1, Pallas kernels, per_device(): call(spectrum_kernel, (shape((rows, 2 * tokens), F32), shape((tokens, wid...  5.94 us
    pallas_call x1, Pallas kernels, per_device(): call(send_kernel, shape((parts, SIDE + TAIL, tokens), BF16), 'vhhh', 'h',...  4 us
    pallas_call x1, Pallas kernels, per_device(): call(momentum_kernel, (shape((weight.shape[0], width), F32), shape((weigh...  2.35 us
  transfers between devices with their start and end apart: 7, of which 5 were waited for; matrix products, arithmetic and copies ran while one was open for 2% of the time, Pallas kernels for 19%

profile of v2, /device:TPU:6, one launch (start us, length us, event | category | flops | bytes accessed | tf_op | source)
XLA Modules:
  0.0 99.6 jit_solution(11346049804604222621)
XLA Ops:
  0.6 4.0 %shard_map.147 = bf16[64,40,128]{2,1,0:T(8,128)(2,1)} custom-call(s32[1,128]{1,0:T(1,128)} %ids_ref.3, bf16[512,2048]{1,0:T(8,128)(2,1)} %embed_hbm.5, bf16[128,2048]{1,0:T(8,128)(2,1)} %bitcast.7, bf16[32,2048]{1,0:T(8,128)(2,1)} %weight_hbm.1), custom_call_target="tpu_custom_call" | custom-call | flops 268435456 | bytes 5242880 | tf_op jit(solution)/shard_map/pallas_call | solution.py:598
  4.6 13.2 %all-to-all-start = ((bf16[64,40,128]{2,1,0:T(8,128)(2,1)}), bf16[64,40,128]{2,1,0:T(8,128)(2,1)S(1)}, u32[]{:S(2)}, u32[]{:S(2)}) async-start(bf16[64,40,128]{2,1,0:T(8,128)(2,1)} %shard_map.147), calls=%async_computation | async-start | bytes 1310720 | tf_op jit(solution)/shard_map/all_to_all | solution.py:578
  17.9 5.9 %shard_map.148 = (f32[2048,256]{1,0:T(8,128)}, bf16[128,2048]{1,0:T(8,128)(2,1)}) custom-call(f32[32,8192]{1,0:T(8,128)} %filters_ref.1, bf16[128,192]{1,0:T(8,128)(2,1)} %constant.15.clone.wide_ref, f32[64,256]{1,0:T(8,128)} %constant.16.clone.twist_ref.twist_hbm, bf16[2,256,256]{2,1,0:T(8,128)(2,1)} %constant.17.clone.mix_ref.mix_hbm, s32[1,128]{1,0:T(1,128)} %ids_ref.3, ...), custom_call_target="tpu_custom_call" | custom-call | flops 5368709120 | bytes 3145728 | tf_op jit(solution)/shard_map/pallas_call | solution.py:614
  23.8 15.5 %all-to-all-done.block_hbm = bf16[64,40,128]{2,1,0:T(8,128)(2,1)S(1)} async-done(((bf16[64,40,128]{2,1,0:T(8,128)(2,1)}), bf16[64,40,128]{2,1,0:T(8,128)(2,1)S(1)}, u32[]{:S(2)}, u32[]{:S(2)}) %all-to-all-start) | async-done | bytes 655392 | tf_op jit(solution)/shard_map/all_to_all | solution.py:578
  39.4 0.8 copy-done.2
  40.2 9.9 %shard_map.149 = (f32[64,8,128]{2,1,0:T(8,128)}, bf16[128,128]{1,0:T(8,128)(2,1)}) custom-call(bf16[64,40,128]{2,1,0:T(8,128)(2,1)} %copy-done.2, bf16[512,2048]{1,0:T(8,128)(2,1)} %embed_hbm.5, f32[2048,256]{1,0:T(8,128)} %get-tuple-element.11.spectrum_hbm, bf16[128,128]{1,0:T(8,128)(2,1)} %constant.18.clone.exact_hbm, ...), custom_call_target="tpu_custom_call" | custom-call | flops 10737418240 | bytes 6291456 | tf_op jit(solution)/shard_map/pallas_call | solution.py:627
  50.1 0.1 collective-permute-start
  50.2 5.1 %all-to-all-start.2 = ((f32[64,8,128]{2,1,0:T(8,128)}), f32[64,8,128]{2,1,0:T(8,128)S(1)}, u32[]{:S(2)}, u32[]{:S(2)}) async-start(f32[64,8,128]{2,1,0:T(8,128)} %get-tuple-element.14), calls=%async_computation.2 | async-start | bytes 524288 | tf_op jit(solution)/shard_map/all_to_all | solution.py:578
  55.3 0.0 copy-start.3
  55.3 0.0 collective-permute-done.other_hbm
  55.3 0.0 copy-start.4
  55.3 0.6 copy-done.4
  55.9 10.5 %shard_map.150 = bf16[64,32,128]{2,1,0:T(8,128)(2,1)} custom-call(bf16[64,40,128]{2,1,0:T(8,128)(2,1)} %copy-done.2, bf16[128,128]{1,0:T(8,128)(2,1)} %copy-done.4, bf16[512,2048]{1,0:T(8,128)(2,1)} %embed_hbm.5, f32[2048,256]{1,0:T(8,128)} %get-tuple-element.11.spectrum_hbm, bf16[128,128]{1,0:T(8,128)(2,1)} %constant.18.clone.exact_hbm, ...), custom_call_target="tpu_custom_call" | custom-call | flops 10737418240 | bytes 6291456 | tf_op jit(solution)/shard_map/pallas_call | solution.py:648
  66.4 2.8 %all-to-all-done.2.grad_hbm = f32[64,8,128]{2,1,0:T(8,128)S(1)} async-done(((f32[64,8,128]{2,1,0:T(8,128)}), f32[64,8,128]{2,1,0:T(8,128)S(1)}, u32[]{:S(2)}, u32[]{:S(2)}) %all-to-all-start.2) | async-done | bytes 262176 | tf_op jit(solution)/shard_map/all_to_all | solution.py:578
  69.3 8.5 %all-to-all-start.1 = ((bf16[64,32,128]{2,1,0:T(8,128)(2,1)}), bf16[64,32,128]{2,1,0:T(8,128)(2,1)S(1)}, u32[]{:S(2)}, u32[]{:S(2)}) async-start(bf16[64,32,128]{2,1,0:T(8,128)(2,1)} %shard_map.150), calls=%async_computation.1 | async-start | bytes 1048576 | tf_op jit(solution)/shard_map/all_to_all | solution.py:578
  77.8 2.4 %shard_map.152 = (f32[32,2048]{1,0:T(8,128)}, f32[32,2048]{1,0:T(8,128)}, bf16[32,2048]{1,0:T(8,128)(2,1)}) custom-call(f32[64,8,128]{2,1,0:T(8,128)} %copy-done.1, f32[32,2048]{1,0:T(8,128)} %bitcast.8, f32[32,2048]{1,0:T(8,128)} %bitcast.9), custom_call_target="tpu_custom_call" | custom-call | flops 1048576 | bytes 2097152 | tf_op jit(solution)/shard_map/pallas_call | solution.py:669
  80.1 1.5 %collective-permute-start.2 = (bf16[32,2048]{1,0:T(8,128)(2,1)}, bf16[32,2048]{1,0:T(8,128)(2,1)S(1)}, u32[]{:S(2)}, u32[]{:S(2)}) collective-permute-start(bf16[32,2048]{1,0:T(8,128)(2,1)} %get-tuple-element.17), channel_id=1, source_target_pairs={{0,128},{64,192},{128,0},{192,64},{1,129},{65,193},{129,1},{193,65... | collective-permute-start | bytes 393224 | tf_op jit(solution)/shard_map/ppermute | solution.py:689
  81.6 0.0 collective-permute-start.1
  81.6 7.5 %collective-permute-done.2 = bf16[32,2048]{1,0:T(8,128)(2,1)S(1)} collective-permute-done((bf16[32,2048]{1,0:T(8,128)(2,1)}, bf16[32,2048]{1,0:T(8,128)(2,1)S(1)}, u32[]{:S(2)}, u32[]{:S(2)}) %collective-permute-start.2) | collective-permute-done | bytes 131104 | tf_op jit(solution)/shard_map/ppermute | solution.py:689
  89.1 1.3 %collective-permute-done.3 = bf16[32,2048]{1,0:T(8,128)(2,1)S(1)} collective-permute-done((bf16[32,2048]{1,0:T(8,128)(2,1)S(1)}, bf16[32,2048]{1,0:T(8,128)(2,1)S(1)}, u32[]{:S(2)}, u32[]{:S(2)}) %collective-permute-start.3) | collective-permute-done | bytes 131104 | tf_op jit(solution)/shard_map/ppermute | solution.py:689
  90.5 1.7 %subtract_convert_fusion = bf16[32,2048]{1,0:T(8,128)(2,1)} fusion(bf16[32,2048]{1,0:T(8,128)(2,1)S(1)} %collective-permute-done.3, bf16[32,2048]{1,0:T(8,128)(2,1)S(1)} %collective-permute-done.2, bf16[32,2048]{1,0:T(8,128)(2,1)S(1)} %collective-permute-done.1, bf16[32,2048]{1,0:T(8,128)(2,1)} %get-tuple-element.17, bf16[32,2048]{1,0:T(8,128)(2,1)S(1)} %copy-done.3), kind=kLoop, calls=%fused_computation | loop fusion | flops 720896 | bytes 786432 | tf_op jit(solution)/shard_map/convert_element_type | solution.py:697
  92.1 4.5 %all-to-all-done.1.conv_hbm = bf16[64,32,128]{2,1,0:T(8,128)(2,1)S(1)} async-done(((bf16[64,32,128]{2,1,0:T(8,128)(2,1)}), bf16[64,32,128]{2,1,0:T(8,128)(2,1)S(1)}, u32[]{:S(2)}, u32[]{:S(2)}) %all-to-all-start.1) | async-done | bytes 524320 | tf_op jit(solution)/shard_map/all_to_all | solution.py:578
  96.6 0.8 copy-done
  97.4 2.1 %shard_map.151 = bf16[128,2048]{1,0:T(8,128)(2,1)} custom-call(bf16[64,32,128]{2,1,0:T(8,128)(2,1)} %copy-done, bf16[128,2048]{1,0:T(8,128)(2,1)} %get-tuple-element.13.inputs_hbm), custom_call_target="tpu_custom_call" | custom-call | flops 1048576 | bytes 2097152 | tf_op jit(solution)/shard_map/pallas_call | solution.py:698
  (7 shorter events, 0.0 us)
Async XLA Ops:
  4.6 34.7 %all-to-all-start = ((bf16[64,40,128]{2,1,0:T(8,128)(2,1)}), bf16[64,40,128]{2,1,0:T(8,128)(2,1)S(1)}, u32[]{:S(2)}, u32[]{:S(2)}) async-start(bf16[64,40,128]{2,1,0:T(8,128)(2,1)} %shard_map.147), calls=%async_computation | async-start | bytes 1310720 | tf_op jit(solution)/shard_map/all_to_all | solution.py:578
  39.4 0.8 copy-start.2
  50.1 5.2 %collective-permute-start = (bf16[128,128]{1,0:T(8,128)(2,1)}, bf16[128,128]{1,0:T(8,128)(2,1)S(1)}, u32[]{:S(2)}, u32[]{:S(2)}) collective-permute-start(bf16[128,128]{1,0:T(8,128)(2,1)} %get-tuple-element.12), channel_id=1, source_target_pairs={{0,64},{64,0},{128,192},{192,128},{1,65},{65,1},{129,193},{193,129... | collective-permute-start | bytes 98312 | tf_op jit(solution)/shard_map/ppermute | solution.py:646
  50.2 19.0 %all-to-all-start.2 = ((f32[64,8,128]{2,1,0:T(8,128)}), f32[64,8,128]{2,1,0:T(8,128)S(1)}, u32[]{:S(2)}, u32[]{:S(2)}) async-start(f32[64,8,128]{2,1,0:T(8,128)} %get-tuple-element.14), calls=%async_computation.2 | async-start | bytes 524288 | tf_op jit(solution)/shard_map/all_to_all | solution.py:578
  55.3 35.2 %copy-start.3 = (bf16[32,2048]{1,0:T(8,128)(2,1)S(1)}, bf16[32,2048]{1,0:T(8,128)(2,1)}, u32[]{:S(2)}) copy-start(bf16[32,2048]{1,0:T(8,128)(2,1)} %weight_hbm.1) | copy-start | bytes 393220
  55.3 0.6 copy-start.4
  69.3 8.5 %copy-start.1 = (f32[64,8,128]{2,1,0:T(8,128)}, f32[64,8,128]{2,1,0:T(8,128)S(1)}, u32[]{:S(2)}) copy-start(f32[64,8,128]{2,1,0:T(8,128)S(1)} %all-to-all-done.2.grad_hbm) | copy-start | bytes 786436
  69.3 27.3 %all-to-all-start.1 = ((bf16[64,32,128]{2,1,0:T(8,128)(2,1)}), bf16[64,32,128]{2,1,0:T(8,128)(2,1)S(1)}, u32[]{:S(2)}, u32[]{:S(2)}) async-start(bf16[64,32,128]{2,1,0:T(8,128)(2,1)} %shard_map.150), calls=%async_computation.1 | async-start | bytes 1048576 | tf_op jit(solution)/shard_map/all_to_all | solution.py:578
  80.1 9.0 %collective-permute-start.2 = (bf16[32,2048]{1,0:T(8,128)(2,1)}, bf16[32,2048]{1,0:T(8,128)(2,1)S(1)}, u32[]{:S(2)}, u32[]{:S(2)}) collective-permute-start(bf16[32,2048]{1,0:T(8,128)(2,1)} %get-tuple-element.17), channel_id=1, source_target_pairs={{0,128},{64,192},{128,0},{192,64},{1,129},{65,193},{129,1},{193,65... | collective-permute-start | bytes 393224 | tf_op jit(solution)/shard_map/ppermute | solution.py:689
  81.6 7.5 %collective-permute-start.1 = (bf16[32,2048]{1,0:T(8,128)(2,1)}, bf16[32,2048]{1,0:T(8,128)(2,1)S(1)}, u32[]{:S(2)}, u32[]{:S(2)}) collective-permute-start(bf16[32,2048]{1,0:T(8,128)(2,1)} %get-tuple-element.17), channel_id=1, source_target_pairs={{0,64},{64,0},{128,192},{192,128},{1,65},{65,1},{129,193},{193,129... | collective-permute-start | bytes 393224 | tf_op jit(solution)/shard_map/ppermute | solution.py:689
  89.1 1.3 %collective-permute-start.3 = (bf16[32,2048]{1,0:T(8,128)(2,1)S(1)}, bf16[32,2048]{1,0:T(8,128)(2,1)S(1)}, u32[]{:S(2)}, u32[]{:S(2)}) collective-permute-start(bf16[32,2048]{1,0:T(8,128)(2,1)S(1)} %collective-permute-done.2), channel_id=1, source_target_pairs={{0,64},{64,0},{128,192},{192,128},{1,65},{65,1},{129,193},{193,129... | collective-permute-start | bytes 393224 | tf_op jit(solution)/shard_map/ppermute | solution.py:689
  96.6 0.8 copy-start

commit v3 on v2

--- a/solution.py
+++ b/solution.py
@@ -16,13 +16,12 @@
 F32 = jnp.float32
 BF16 = jnp.bfloat16
 LANES = 128
-GROUP = 16
-STEP = 8
+GROUP = 32
+STEP = 32
 TAIL = 8
 SENT = 6
 HALVES = 4
 SIDE = 32
-VMEM_LIMIT = 58 * 1024 * 1024
 CHUNKS = 2
 TABLES = 4
 
@@ -278,27 +277,28 @@
     wait_all(sent)
 
 
-def read_ids(block_ref, first):
-    tails = [block_ref[first + k].astype(F32)[SIDE + SENT :] for k in range(2)]
-    both = jnp.concatenate(tails, axis=1)
+def read_ids(tails_ref, first):
+    start = pl.multiple_of(first * TAIL, 2 * TAIL)
+    tails = tails_ref[pl.ds(start, 2 * TAIL), :].astype(F32)
+    both = jnp.concatenate([tails[SENT:TAIL], tails[TAIL + SENT :]], axis=1)
     high, low = both[0:1], both[1:2]
     index = lax.broadcasted_iota(jnp.int32, (LANES, 2 * LANES), 0).astype(F32)
     return high, jnp.where(index == low, 1.0, 0.0).astype(BF16)
 
 
 def forward_kernel(
-    block_hbm, other_hbm, embed_hbm, spectrum_hbm, exact_hbm, twist_hbm, mix_hbm, back_hbm,
+    tails_hbm, other_hbm, embed_hbm, spectrum_hbm, exact_hbm, twist_hbm, mix_hbm, back_hbm,
     out_hbm,
-    block_ref, other_ref, embed_ref, spectrum_ref, exact_ref, twist_ref, mix_ref, back_ref,
+    tails_ref, other_ref, embed_ref, spectrum_ref, exact_ref, twist_ref, mix_ref, back_ref,
     values_ref, weight_ref, table_ref, out_ref, sems,
 ):
-    peers = block_ref.shape[0]
+    peers = tails_ref.shape[0] // TAIL
     vocab, width = embed_ref.shape
     groups = SIDE // GROUP
     half = width // 2
-    block_copy, other_copy, embed_first, embed_second = start_all(
-        [
-            (block_hbm, block_ref),
+    tails_copy, other_copy, embed_first, embed_second = start_all(
+        [
+            (tails_hbm, tails_ref),
             (other_hbm, other_ref),
             (embed_hbm.at[:, pl.ds(0, half)], embed_ref.at[:, pl.ds(0, half)]),
             (embed_hbm.at[:, pl.ds(half, half)], embed_ref.at[:, pl.ds(half, half)]),
@@ -323,7 +323,7 @@
         sems,
         4 + TABLES,
     )
-    block_copy.wait()
+    tails_copy.wait()
     other_copy.wait()
     late = second_core()
 
@@ -331,10 +331,12 @@
     def _(step):
         others = other_ref[pl.ds(pl.multiple_of(step * 2 * STEP, 2 * STEP), 2 * STEP), :]
         others = others.astype(F32)
+        tails = tails_ref[pl.ds(pl.multiple_of(step * TAIL * STEP, TAIL * STEP), TAIL * STEP), :]
+        tails = tails.astype(F32)
         for k in range(STEP):
             peer = step * STEP + k
-            tail = block_ref[peer].astype(F32)[SIDE : SIDE + SENT]
-            mine, other = tail[4:], others[2 * k : 2 * k + 2]
+            tail = tails[k * TAIL : (k + 1) * TAIL]
+            mine, other = tail[4:SENT], others[2 * k : 2 * k + 2]
             part = jnp.concatenate(
                 [tail[:4], jnp.where(late, other, mine), jnp.where(late, mine, other)], axis=0
             )
@@ -360,7 +362,7 @@
     def _(step):
         for k in range(0, STEP, 2):
             first = step * STEP + k
-            high, picks = read_ids(block_ref, first)
+            high, picks = read_ids(tails_ref, first)
             every = mm(table_ref[...], picks)
             columns = every[:SIDE]
             for part in range(1, vocab // LANES):
@@ -388,18 +390,17 @@
 
 
 def backward_kernel(
-    block_hbm, embed_hbm, spectrum_hbm, exact_hbm, twist_hbm, mix_hbm, back_hbm,
-    out_hbm, other_hbm,
-    block_ref, embed_ref, spectrum_ref, exact_ref, twist_ref, mix_ref, back_ref,
-    values_ref, sums_ref, out_ref, other_ref, sems,
+    block_ref, embed_hbm, spectrum_hbm, exact_hbm, twist_hbm, mix_hbm, back_hbm,
+    out_hbm, other_hbm, tails_hbm,
+    embed_ref, spectrum_ref, exact_ref, twist_ref, mix_ref, back_ref,
+    values_ref, sums_ref, out_ref, other_ref, tails_ref, sems,
 ):
     peers = block_ref.shape[0]
     vocab, width = embed_ref.shape
     groups = SIDE // GROUP
     scaling = 1.0 / math.sqrt(peers * LANES)
-    block_copies = start_all(
-        [
-            (block_hbm, block_ref),
+    table_copies = start_all(
+        [
             (exact_hbm, exact_ref),
             (twist_hbm, twist_ref),
             (mix_hbm, mix_ref),
@@ -407,7 +408,6 @@
         ],
         sems,
     )
-    block_copies[0].wait()
     spectrum_copies = start_all(
         [
             (spectrum_hbm.at[group_rows(k, peers)], spectrum_ref.at[group_rows(k, peers)])
@@ -420,18 +420,24 @@
 
     @pl.loop(0, peers // STEP)
     def _(step):
-        others = []
+        others, tails = [], []
         for k in range(STEP):
             peer = step * STEP + k
             part = block_ref[peer].astype(F32)
             values_ref[pl.ds(pl.multiple_of(peer * SIDE, SIDE), SIDE), :] = part[:SIDE]
             others.append(part[SIDE + 4 : SIDE + SENT])
+            tails.append(part[SIDE:])
         other_ref[pl.ds(pl.multiple_of(step * 2 * STEP, 2 * STEP), 2 * STEP), :] = (
             jnp.concatenate(others, axis=0).astype(BF16)
         )
-
-    copies = start_all([(other_ref, other_hbm)], sems, 2 + TABLES + groups)
-    wait_all(block_copies[1:])
+        tails_ref[pl.ds(pl.multiple_of(step * TAIL * STEP, TAIL * STEP), TAIL * STEP), :] = (
+            jnp.concatenate(tails, axis=0).astype(BF16)
+        )
+
+    copies = start_all(
+        [(other_ref, other_hbm), (tails_ref, tails_hbm)], sems, 2 + TABLES + groups
+    )
+    wait_all(table_copies)
     convolve(
         values_ref, spectrum_ref, (exact_ref, twist_ref, mix_ref, back_ref), -1.0, spectrum_copies
     )
@@ -442,7 +448,7 @@
         total = sums_ref[...]
         for k in range(0, STEP, 2):
             first = step * STEP + k
-            high, picks = read_ids(block_ref, first)
+            high, picks = read_ids(tails_ref, first)
             rows = values_ref[pl.ds(pl.multiple_of(first * SIDE, 2 * SIDE), 2 * SIDE), :]
             columns = jnp.concatenate([rows[:SIDE], rows[SIDE:]], axis=1)
             masked = [jnp.where(high == part, columns, 0.0) for part in range(vocab // LANES)]
@@ -473,7 +479,7 @@
                 for k in range(HALVES):
                     out_ref[block * HALVES + k] = turned[k * SIDE : k * SIDE + 8]
         rows = pl.ds(chunk * blocks * HALVES, blocks * HALVES)
-        copies += start_all([(out_ref.at[rows], out_hbm.at[rows])], sems, 3 + TABLES + groups + chunk)
+        copies += start_all([(out_ref.at[rows], out_hbm.at[rows])], sems, 4 + TABLES + groups + chunk)
     wait_all(copies)
 
 
@@ -528,29 +534,23 @@
     wait_all(sent)
 
 
-def output_kernel(conv_hbm, inputs_hbm, out_hbm, conv_ref, inputs_ref, out_ref, sems):
-    peers = conv_ref.shape[0]
+def output_kernel(conv_ref, inputs_hbm, out_hbm, inputs_ref, out_ref, sems):
     width = out_ref.shape[1]
     blocks = width // LANES // CHUNKS
     copies = []
     for chunk in range(CHUNKS):
         lane = lane_span(chunk, width)
-        rows = peer_span(chunk, peers)
-        pairs = [
-            (conv_hbm.at[rows], conv_ref.at[rows]),
-            (inputs_hbm.at[:, lane], inputs_ref.at[:, lane]),
-        ]
-        copies.append(start_all(pairs, sems, 2 * chunk))
+        copies += start_all([(inputs_hbm.at[:, lane], inputs_ref.at[:, lane])], sems, chunk)
     sent = []
     for chunk in range(CHUNKS):
-        wait_all(copies[chunk])
+        copies[chunk].wait()
         for block in range(chunk * blocks, (chunk + 1) * blocks):
             lane = slice(block * LANES, (block + 1) * LANES)
             rows = [conv_ref[block * HALVES + k].astype(F32) for k in range(HALVES)]
             conv = jnp.concatenate(rows, axis=0).T
             out_ref[:, lane] = (inputs_ref[:, lane].astype(F32) * conv).astype(BF16)
         lane = lane_span(chunk, width)
-        sent += start_all([(out_ref.at[:, lane], out_hbm.at[:, lane])], sems, 2 * CHUNKS + chunk)
+        sent += start_all([(out_ref.at[:, lane], out_hbm.at[:, lane])], sems, CHUNKS + chunk)
     wait_all(sent)
 
 
@@ -561,7 +561,7 @@
     ]
 
 
-def call(kernel, out_shape, ins, outs, scratch=(), flops=0, moved=0):
+def call(kernel, out_shape, ins, outs, scratch=(), flops=0, moved=0, limit=60817408):
     out_specs = spaces(outs)
     return pl.pallas_call(
         kernel,
@@ -569,7 +569,7 @@
         in_specs=spaces(ins),
         out_specs=out_specs if len(outs) > 1 else out_specs[0],
         scratch_shapes=list(scratch),
-        compiler_params=pltpu.CompilerParams(vmem_limit_bytes=VMEM_LIMIT),
+        compiler_params=pltpu.CompilerParams(vmem_limit_bytes=limit),
         cost_estimate=pl.CostEstimate(flops=flops, bytes_accessed=moved, transcendentals=0),
     )
 
@@ -623,14 +623,18 @@
         ],
         flops=5 << 30,
         moved=3 << 20,
+        limit=16777216,
     )(filters, tables["wide"], tables["twist"], tables["mix"], ids, embed)
-    gradient, other = call(
+    gradient, other, tails = call(
         backward_kernel,
-        (shape((parts, 8, tokens), F32), shape((2 * parts, tokens), BF16)),
-        "ahhhhhh",
-        "hh",
-        [
-            pltpu.VMEM((parts, SIDE + TAIL, tokens), BF16),
+        (
+            shape((parts, 8, tokens), F32),
+            shape((2 * parts, tokens), BF16),
+            shape((TAIL * parts, tokens), BF16),
+        ),
+        "vhhhhhh",
+        "hhh",
+        [
             pltpu.VMEM((vocab, width), BF16),
             pltpu.VMEM((rows, 2 * tokens), F32),
             *table_scratch,
@@ -638,10 +642,12 @@
             pltpu.VMEM((LANES, LANES), F32),
             pltpu.VMEM((parts, 8, tokens), F32),
             pltpu.VMEM((2 * parts, tokens), BF16),
-            pltpu.SemaphoreType.DMA((3 + TABLES + groups + CHUNKS,)),
+            pltpu.VMEM((TAIL * parts, tokens), BF16),
+            pltpu.SemaphoreType.DMA((4 + TABLES + groups + CHUNKS,)),
         ],
         flops=10 << 30,
         moved=6 << 20,
+        limit=62820000,
     )(block, embed, spectrum, *convolve_tables)
     other = lax.ppermute(other, "dp", [(source, source ^ 1) for source in range(replicas)])
     gradient = exchange(gradient)
@@ -651,7 +657,7 @@
         "aahhhhhh",
         "h",
         [
-            pltpu.VMEM((parts, SIDE + TAIL, tokens), BF16),
+            pltpu.VMEM((TAIL * parts, tokens), BF16),
             pltpu.VMEM((2 * parts, tokens), BF16),
             pltpu.VMEM((vocab, width), BF16),
             pltpu.VMEM((rows, 2 * tokens), F32),
@@ -664,7 +670,8 @@
         ],
         flops=10 << 30,
         moved=6 << 20,
-    )(block, other, embed, spectrum, *convolve_tables)
+        limit=60817408,
+    )(tails, other, embed, spectrum, *convolve_tables)
     convolved = exchange(convolved)
     updated, residue, quantized = call(
         momentum_kernel,
@@ -684,6 +691,7 @@
         ],
         flops=1 << 20,
         moved=2 << 20,
+        limit=60817408,
     )(gradient, momentum[0], feedback[0])
     def swap(values, flip):
         return lax.ppermute(values, "dp", [(source, source ^ flip) for source in range(replicas)])
@@ -698,16 +706,16 @@
     output = call(
         output_kernel,
         shape((tokens, width), BF16),
-        "aa",
+        "va",
         "h",
         [
-            pltpu.VMEM((parts, channels, tokens), BF16),
             pltpu.VMEM((tokens, width), BF16),
             pltpu.VMEM((tokens, width), BF16),
-            pltpu.SemaphoreType.DMA((3 * CHUNKS,)),
+            pltpu.SemaphoreType.DMA((2 * CHUNKS,)),
         ],
         flops=1 << 20,
         moved=2 << 20,
+        limit=16777216,
     )(convolved, inputs)
     return (output[None], updated[None], residue[None], new_weight)
 

time: 100 us -> 96.2 us (0.962)
  Pallas kernels: 34.8 us -> 29.5 us
  waiting for transfers between devices: 31.7 us -> 33.1 us
  starting transfers between devices: 28.4 us -> 27.3 us
    pallas_call x1, Pallas kernels: 5.94 us -> 3.14 us  [per_device(): call(spectrum_kernel, (shape((rows, 2 * tokens), F32), shape((tokens, wid...]
    all_to_all x3, waiting for transfers between devices: 22.9 us -> 24.3 us  [exchange(): lax.all_to_all(values, 'seq', split_axis=0, concat_axis=0, tiled=True)]
    pallas_call x1, Pallas kernels: 10.5 us -> 9.24 us  [per_device(): call(forward_kernel, shape((parts, channels, tokens), BF16), 'aahhhhhh',...]
    all_to_all x3, starting transfers between devices: 26.8 us -> 25.7 us  [exchange(): lax.all_to_all(values, 'seq', split_axis=0, concat_axis=0, tiled=True)]
    pallas_call x1, Pallas kernels: 2.08 us -> 1.06 us  [per_device(): call(output_kernel, shape((tokens, width), BF16), 'va', 'h', [pltpu.VMEM(...]
    unnamed x10 -> x20, local copies, waits for them, and re-layouts: 2.24 us -> 3.19 us
  transfers between devices with their start and end apart: 7 -> 7, of which waited for: 5 -> 5; matrix products, arithmetic and copies ran while one was open for 2% -> 2% of each run, Pallas kernels for 19% -> 15%
where the time goes in v3:
time: 96.2 us; the launch traced here: 95.8 us
  waiting for transfers between devices  33.1 us (34%)
  Pallas kernels  29.5 us (31%)
  starting transfers between devices  27.3 us (28%)
  local copies, waits for them, and re-layouts  3.19 us (3%)
  other arithmetic  1.65 us (2%)
  between operations  0.99 us (1%)
    all_to_all x3, starting transfers between devices, exchange(): lax.all_to_all(values, 'seq', split_axis=0, concat_axis=0, tiled=True)  25.7 us
    all_to_all x3, waiting for transfers between devices, exchange(): lax.all_to_all(values, 'seq', split_axis=0, concat_axis=0, tiled=True)  24.3 us
    pallas_call x1, Pallas kernels, per_device(): call(backward_kernel, (shape((parts, 8, tokens), F32), shape((2 * parts,...  9.59 us
    pallas_call x1, Pallas kernels, per_device(): call(forward_kernel, shape((parts, channels, tokens), BF16), 'aahhhhhh',...  9.24 us
    ppermute x3, waiting for transfers between devices, swap(): lax.ppermute(values, 'dp', [(source, source ^ flip) for source in range(r...  8.86 us
    pallas_call x1, Pallas kernels, per_device(): call(send_kernel, shape((parts, SIDE + TAIL, tokens), BF16), 'vhhh', 'h',...  4.15 us
    unnamed x20, local copies, waits for them, and re-layouts  3.19 us
    pallas_call x1, Pallas kernels, per_device(): call(spectrum_kernel, (shape((rows, 2 * tokens), F32), shape((tokens, wid...  3.14 us
  transfers between devices with their start and end apart: 7, of which 5 were waited for; matrix products, arithmetic and copies ran while one was open for 2% of the time, Pallas kernels for 15%

profile of v3, /device:TPU:6, one launch (start us, length us, event | category | flops | bytes accessed | tf_op | source)
XLA Modules:
  0.0 95.8 jit_solution(7719455832708216145)
XLA Ops:
  0.6 0.0 copy-start
  0.7 0.0 copy-start.3
  0.7 0.0 copy-start.4
  0.7 0.0 copy-start.5
  0.7 4.2 %shard_map.147 = bf16[64,40,128]{2,1,0:T(8,128)(2,1)} custom-call(s32[1,128]{1,0:T(1,128)} %ids_ref.3, bf16[512,2048]{1,0:T(8,128)(2,1)} %embed_hbm.5, bf16[128,2048]{1,0:T(8,128)(2,1)} %bitcast.7, bf16[32,2048]{1,0:T(8,128)(2,1)} %weight_hbm.1), custom_call_target="tpu_custom_call" | custom-call | flops 268435456 | bytes 5242880 | tf_op jit(solution)/shard_map/pallas_call | solution.py:598
  4.9 13.4 %all-to-all-start = ((bf16[64,40,128]{2,1,0:T(8,128)(2,1)}), bf16[64,40,128]{2,1,0:T(8,128)(2,1)}, u32[]{:S(2)}, u32[]{:S(2)}) async-start(bf16[64,40,128]{2,1,0:T(8,128)(2,1)} %shard_map.147), calls=%async_computation | async-start | bytes 1310720 | tf_op jit(solution)/shard_map/all_to_all | solution.py:578
  18.3 1.2 %copy-done.2 = f32[32,8192]{1,0:T(8,128)S(1)} copy-done((f32[32,8192]{1,0:T(8,128)S(1)}, f32[32,8192]{1,0:T(8,128)}, u32[]{:S(2)}) %copy-start.2) | copy-done | bytes 1048600
  19.5 3.1 %shard_map.148 = (f32[2048,256]{1,0:T(8,128)S(1)}, bf16[128,2048]{1,0:T(8,128)(2,1)S(1)}) custom-call(f32[32,8192]{1,0:T(8,128)S(1)} %copy-done.2, bf16[128,192]{1,0:T(8,128)(2,1)S(1)} %copy-done.5, f32[64,256]{1,0:T(8,128)S(1)} %copy-done.4, bf16[2,256,256]{2,1,0:T(8,128)(2,1)S(1)} %copy-done.3, s32[1,128]{1,0:T(1,128)S(1)} %copy-done.1, ...), custom_call_target="tpu_custom_call" | custom-call | flops 5368709120 | bytes 3145728 | tf_op jit(solution)/shard_map/pallas_call | solution.py:614
  22.7 1.3 %copy-done.6 = f32[2048,256]{1,0:T(8,128)} copy-done((f32[2048,256]{1,0:T(8,128)}, f32[2048,256]{1,0:T(8,128)S(1)}, u32[]{:S(2)}) %copy-start.6) | copy-done | bytes 2097176
  24.0 15.7 %all-to-all-done.block_ref = bf16[64,40,128]{2,1,0:T(8,128)(2,1)} async-done(((bf16[64,40,128]{2,1,0:T(8,128)(2,1)}), bf16[64,40,128]{2,1,0:T(8,128)(2,1)}, u32[]{:S(2)}, u32[]{:S(2)}) %all-to-all-start) | async-done | bytes 655392 | tf_op jit(solution)/shard_map/all_to_all | solution.py:578
  39.7 9.6 %shard_map.149 = (f32[64,8,128]{2,1,0:T(8,128)}, bf16[128,128]{1,0:T(8,128)(2,1)}, bf16[512,128]{1,0:T(8,128)(2,1)}) custom-call(bf16[64,40,128]{2,1,0:T(8,128)(2,1)} %all-to-all-done.block_ref, bf16[512,2048]{1,0:T(8,128)(2,1)} %embed_hbm.5, f32[2048,256]{1,0:T(8,128)} %copy-done.6, bf16[128,128]{1,0:T(8,128)(2,1)} %constant.18.clone.exact_hbm, ...), custom_call_target="tpu_custom_call" | custom-call | flops 10737418240 | bytes 6291456 | tf_op jit(solution)/shard_map/pallas_call | solution.py:628
  49.3 0.1 collective-permute-start
  49.4 5.1 %all-to-all-start.2 = ((f32[64,8,128]{2,1,0:T(8,128)}), f32[64,8,128]{2,1,0:T(8,128)S(1)}, u32[]{:S(2)}, u32[]{:S(2)}) async-start(f32[64,8,128]{2,1,0:T(8,128)} %get-tuple-element.16), calls=%async_computation.2 | async-start | bytes 524288 | tf_op jit(solution)/shard_map/all_to_all | solution.py:578
  54.5 0.6 copy-done.9
  55.1 9.2 %shard_map.150 = bf16[64,32,128]{2,1,0:T(8,128)(2,1)} custom-call(bf16[512,128]{1,0:T(8,128)(2,1)} %get-tuple-element.13.tails_hbm, bf16[128,128]{1,0:T(8,128)(2,1)} %copy-done.9, bf16[512,2048]{1,0:T(8,128)(2,1)} %embed_hbm.5, f32[2048,256]{1,0:T(8,128)} %copy-done.6, bf16[128,128]{1,0:T(8,128)(2,1)} %constant.18.clone.exact_hbm, ...), custom_call_target="tpu_custom_call" | custom-call | flops 10737418240 | bytes 6291456 | tf_op jit(solution)/shard_map/pallas_call | solution.py:654
  64.3 4.1 %all-to-all-done.2.grad_hbm = f32[64,8,128]{2,1,0:T(8,128)S(1)} async-done(((f32[64,8,128]{2,1,0:T(8,128)}), f32[64,8,128]{2,1,0:T(8,128)S(1)}, u32[]{:S(2)}, u32[]{:S(2)}) %all-to-all-start.2) | async-done | bytes 262176 | tf_op jit(solution)/shard_map/all_to_all | solution.py:578
  68.4 7.2 %all-to-all-start.1 = ((bf16[64,32,128]{2,1,0:T(8,128)(2,1)}), bf16[64,32,128]{2,1,0:T(8,128)(2,1)S(1)}, u32[]{:S(2)}, u32[]{:S(2)}) async-start(bf16[64,32,128]{2,1,0:T(8,128)(2,1)} %shard_map.150), calls=%async_computation.1 | async-start | bytes 1048576 | tf_op jit(solution)/shard_map/all_to_all | solution.py:578
  75.7 2.4 %shard_map.152 = (f32[32,2048]{1,0:T(8,128)}, f32[32,2048]{1,0:T(8,128)}, bf16[32,2048]{1,0:T(8,128)(2,1)}) custom-call(f32[64,8,128]{2,1,0:T(8,128)} %copy-done.7, f32[32,2048]{1,0:T(8,128)} %bitcast.8, f32[32,2048]{1,0:T(8,128)} %bitcast.9), custom_call_target="tpu_custom_call" | custom-call | flops 1048576 | bytes 2097152 | tf_op jit(solution)/shard_map/pallas_call | solution.py:676
  78.0 1.5 %collective-permute-start.2 = (bf16[32,2048]{1,0:T(8,128)(2,1)}, bf16[32,2048]{1,0:T(8,128)(2,1)S(1)}, u32[]{:S(2)}, u32[]{:S(2)}) collective-permute-start(bf16[32,2048]{1,0:T(8,128)(2,1)} %get-tuple-element.19), channel_id=1, source_target_pairs={{0,128},{64,192},{128,0},{192,64},{1,129},{65,193},{129,1},{193,65... | collective-permute-start | bytes 393224 | tf_op jit(solution)/shard_map/ppermute | solution.py:697
  79.5 7.5 %collective-permute-done.2 = bf16[32,2048]{1,0:T(8,128)(2,1)S(1)} collective-permute-done((bf16[32,2048]{1,0:T(8,128)(2,1)}, bf16[32,2048]{1,0:T(8,128)(2,1)S(1)}, u32[]{:S(2)}, u32[]{:S(2)}) %collective-permute-start.2) | collective-permute-done | bytes 131104 | tf_op jit(solution)/shard_map/ppermute | solution.py:697
  87.1 1.3 %collective-permute-done.3 = bf16[32,2048]{1,0:T(8,128)(2,1)S(1)} collective-permute-done((bf16[32,2048]{1,0:T(8,128)(2,1)S(1)}, bf16[32,2048]{1,0:T(8,128)(2,1)S(1)}, u32[]{:S(2)}, u32[]{:S(2)}) %collective-permute-start.3) | collective-permute-done | bytes 131104 | tf_op jit(solution)/shard_map/ppermute | solution.py:697
  88.4 1.7 %subtract_convert_fusion = bf16[32,2048]{1,0:T(8,128)(2,1)} fusion(bf16[32,2048]{1,0:T(8,128)(2,1)S(1)} %collective-permute-done.3, bf16[32,2048]{1,0:T(8,128)(2,1)S(1)} %collective-permute-done.2, bf16[32,2048]{1,0:T(8,128)(2,1)S(1)} %collective-permute-done.1, bf16[32,2048]{1,0:T(8,128)(2,1)} %get-tuple-element.19, bf16[32,2048]{1,0:T(8,128)(2,1)S(1)} %copy-done.8), kind=kLoop, calls=%fused_computation | loop fusion | flops 720896 | bytes 786432 | tf_op jit(solution)/shard_map/convert_element_type | solution.py:705
  90.1 4.5 %all-to-all-done.1.conv_ref = bf16[64,32,128]{2,1,0:T(8,128)(2,1)S(1)} async-done(((bf16[64,32,128]{2,1,0:T(8,128)(2,1)}), bf16[64,32,128]{2,1,0:T(8,128)(2,1)S(1)}, u32[]{:S(2)}, u32[]{:S(2)}) %all-to-all-start.1) | async-done | bytes 524320 | tf_op jit(solution)/shard_map/all_to_all | solution.py:578
  94.5 1.1 %shard_map.151 = bf16[128,2048]{1,0:T(8,128)(2,1)} custom-call(bf16[64,32,128]{2,1,0:T(8,128)(2,1)S(1)} %all-to-all-done.1.conv_ref, bf16[128,2048]{1,0:T(8,128)(2,1)S(1)} %get-tuple-element.15.inputs_hbm), custom_call_target="tpu_custom_call" | custom-call | flops 1048576 | bytes 2097152 | tf_op jit(solution)/shard_map/pallas_call | solution.py:706
  (17 shorter events, 0.0 us)
Async XLA Ops:
  0.6 17.6 %copy-start = (bf16[512,2048]{1,0:T(8,128)(2,1)S(1)}, bf16[512,2048]{1,0:T(8,128)(2,1)}, u32[]{:S(2)}) copy-start(bf16[512,2048]{1,0:T(8,128)(2,1)} %embed_hbm.5) | copy-start | bytes 6291460
  0.6 17.6 %copy-start.1 = (s32[1,128]{1,0:T(1,128)S(1)}, s32[1,128]{1,0:T(1,128)}, u32[]{:S(2)}) copy-start(s32[1,128]{1,0:T(1,128)} %ids_ref.3) | copy-start | bytes 1540
  0.7 17.6 %copy-start.3 = (bf16[2,256,256]{2,1,0:T(8,128)(2,1)S(1)}, bf16[2,256,256]{2,1,0:T(8,128)(2,1)}, u32[]{:S(2)}) copy-start(bf16[2,256,256]{2,1,0:T(8,128)(2,1)} %constant.17.clone.mix_ref.mix_hbm) | copy-start | bytes 786436
  0.7 17.6 %copy-start.4 = (f32[64,256]{1,0:T(8,128)S(1)}, f32[64,256]{1,0:T(8,128)}, u32[]{:S(2)}) copy-start(f32[64,256]{1,0:T(8,128)} %constant.16.clone.twist_ref.twist_hbm) | copy-start | bytes 196612
  0.7 17.6 %copy-start.5 = (bf16[128,192]{1,0:T(8,128)(2,1)S(1)}, bf16[128,192]{1,0:T(8,128)(2,1)}, u32[]{:S(2)}) copy-start(bf16[128,192]{1,0:T(8,128)(2,1)} %constant.15.clone.wide_ref) | copy-start | bytes 147460
  4.9 34.8 %all-to-all-start = ((bf16[64,40,128]{2,1,0:T(8,128)(2,1)}), bf16[64,40,128]{2,1,0:T(8,128)(2,1)}, u32[]{:S(2)}, u32[]{:S(2)}) async-start(bf16[64,40,128]{2,1,0:T(8,128)(2,1)} %shard_map.147), calls=%async_computation | async-start | bytes 1310720 | tf_op jit(solution)/shard_map/all_to_all | solution.py:578
  18.3 1.2 %copy-start.2 = (f32[32,8192]{1,0:T(8,128)S(1)}, f32[32,8192]{1,0:T(8,128)}, u32[]{:S(2)}) copy-start(f32[32,8192]{1,0:T(8,128)} %filters_ref.1) | copy-start | bytes 3145732
  22.7 1.3 %copy-start.6 = (f32[2048,256]{1,0:T(8,128)}, f32[2048,256]{1,0:T(8,128)S(1)}, u32[]{:S(2)}) copy-start(f32[2048,256]{1,0:T(8,128)S(1)} %get-tuple-element.12.spectrum_hbm) | copy-start | bytes 6291460
  49.3 5.2 %collective-permute-start = (bf16[128,128]{1,0:T(8,128)(2,1)}, bf16[128,128]{1,0:T(8,128)(2,1)S(1)}, u32[]{:S(2)}, u32[]{:S(2)}) collective-permute-start(bf16[128,128]{1,0:T(8,128)(2,1)} %get-tuple-element.14), channel_id=1, source_target_pairs={{0,64},{64,0},{128,192},{192,128},{1,65},{65,1},{129,193},{193,129... | collective-permute-start | bytes 98312 | tf_op jit(solution)/shard_map/ppermute | solution.py:652
  49.4 19.1 %all-to-all-start.2 = ((f32[64,8,128]{2,1,0:T(8,128)}), f32[64,8,128]{2,1,0:T(8,128)S(1)}, u32[]{:S(2)}, u32[]{:S(2)}) async-start(f32[64,8,128]{2,1,0:T(8,128)} %get-tuple-element.16), calls=%async_computation.2 | async-start | bytes 524288 | tf_op jit(solution)/shard_map/all_to_all | solution.py:578
  54.5 0.6 copy-start.9
  55.1 33.3 %copy-start.8 = (bf16[32,2048]{1,0:T(8,128)(2,1)S(1)}, bf16[32,2048]{1,0:T(8,128)(2,1)}, u32[]{:S(2)}) copy-start(bf16[32,2048]{1,0:T(8,128)(2,1)} %weight_hbm.1) | copy-start | bytes 393220
  68.4 7.2 %copy-start.7 = (f32[64,8,128]{2,1,0:T(8,128)}, f32[64,8,128]{2,1,0:T(8,128)S(1)}, u32[]{:S(2)}) copy-start(f32[64,8,128]{2,1,0:T(8,128)S(1)} %all-to-all-done.2.grad_hbm) | copy-start | bytes 786436
  68.4 26.1 %all-to-all-start.1 = ((bf16[64,32,128]{2,1,0:T(8,128)(2,1)}), bf16[64,32,128]{2,1,0:T(8,128)(2,1)S(1)}, u32[]{:S(2)}, u32[]{:S(2)}) async-start(bf16[64,32,128]{2,1,0:T(8,128)(2,1)} %shard_map.150), calls=%async_computation.1 | async-start | bytes 1048576 | tf_op jit(solution)/shard_map/all_to_all | solution.py:578
  78.0 9.0 %collective-permute-start.2 = (bf16[32,2048]{1,0:T(8,128)(2,1)}, bf16[32,2048]{1,0:T(8,128)(2,1)S(1)}, u32[]{:S(2)}, u32[]{:S(2)}) collective-permute-start(bf16[32,2048]{1,0:T(8,128)(2,1)} %get-tuple-element.19), channel_id=1, source_target_pairs={{0,128},{64,192},{128,0},{192,64},{1,129},{65,193},{129,1},{193,65... | collective-permute-start | bytes 393224 | tf_op jit(solution)/shard_map/ppermute | solution.py:697
  79.5 7.5 %collective-permute-start.1 = (bf16[32,2048]{1,0:T(8,128)(2,1)}, bf16[32,2048]{1,0:T(8,128)(2,1)S(1)}, u32[]{:S(2)}, u32[]{:S(2)}) collective-permute-start(bf16[32,2048]{1,0:T(8,128)(2,1)} %get-tuple-element.19), channel_id=1, source_target_pairs={{0,64},{64,0},{128,192},{192,128},{1,65},{65,1},{129,193},{193,129... | collective-permute-start | bytes 393224 | tf_op jit(solution)/shard_map/ppermute | solution.py:697
  87.1 1.3 %collective-permute-start.3 = (bf16[32,2048]{1,0:T(8,128)(2,1)S(1)}, bf16[32,2048]{1,0:T(8,128)(2,1)S(1)}, u32[]{:S(2)}, u32[]{:S(2)}) collective-permute-start(bf16[32,2048]{1,0:T(8,128)(2,1)S(1)} %collective-permute-done.2), channel_id=1, source_target_pairs={{0,64},{64,0},{128,192},{192,128},{1,65},{65,1},{129,193},{193,129... | collective-permute-start | bytes 393224 | tf_op jit(solution)/shard_map/ppermute | solution.py:697

commit v4 on v3

--- a/solution.py
+++ b/solution.py
@@ -32,25 +32,32 @@
     return high, low
 
 
+def packed_mix(table):
+    high, low = split_const(
+        np.block([[table.real, table.imag], [-table.imag, table.real]])
+    )
+    return np.block([[high, low], [high, np.zeros_like(low)]])
+
+
 def transform_tables(outer, inner):
     total = outer * inner
     freq = np.arange(outer)[:, None] + 0.25
     first = np.exp(-2j * np.pi * freq * np.arange(outer)[None, :] / outer)
     twist = np.exp(-2j * np.pi * freq * np.arange(inner)[None, :] / total)
-    second = np.exp(
-        -2j * np.pi * (np.arange(inner)[:, None] * np.arange(inner)[None, :] % inner) / inner
-    )
+    half = inner // 2
+    near, bins = np.arange(half)[:, None], 2 * np.arange(half)[None, :]
+    even = np.exp(-2j * np.pi * (near * bins % inner) / inner)
+    odd = np.exp(-2j * np.pi * (near * (bins + 1) % inner) / inner)
     stage = np.concatenate([first.real, first.imag], axis=0)
     high, low = split_const(stage)
     back_high, back_low = split_const(stage.T)
-    real, imag = second.real, second.imag
-    mix = np.block([[real, imag], [-imag, real]])
+    mixes = [packed_mix(table) for table in (even, odd, even.conj().T, odd.conj().T)]
     return {
         "exact": np.concatenate([high, low], axis=1),
         "wide": np.concatenate([high, high, low], axis=1),
         "back": np.concatenate([back_high, back_high, back_low], axis=1),
         "twist": np.concatenate([twist.real, twist.imag], axis=1).astype(np.float32),
-        "mix": np.stack(split_const(mix)),
+        "mix": np.stack(mixes),
     }
 
 
@@ -63,18 +70,24 @@
     return high, (values - high.astype(F32)).astype(BF16)
 
 
-def mm_wide(values, table_ref):
-    rows = values.shape[0]
-    high, low = halves(values)
-    both = mm(jnp.concatenate([high, low], axis=0), table_ref[0])
-    return both[:rows] + both[rows:] + mm(high, table_ref[1])
+def mm_packed(values, table):
+    both = mm(jnp.concatenate(halves(values), axis=1), table)
+    return both[:, :LANES] + both[:, LANES:]
+
+
+def turn(values):
+    return pltpu.roll(values, LANES // 2, 1)
+
+
+def in_low(values):
+    return lax.broadcasted_iota(jnp.int32, values.shape, 1) < LANES // 2
 
 
 def spread(columns, stage_ref, twist_ref, exact):
     real_twist = twist_ref[:, :LANES]
     imag_twist = twist_ref[:, LANES:]
     outer = real_twist.shape[0]
-    rows = []
+    evens, odds = [], []
     for first in range(0, len(columns), 2):
         pair = jnp.concatenate(columns[first : first + 2], axis=1)
         if exact:
@@ -88,32 +101,32 @@
             lane = slice(which * LANES, (which + 1) * LANES)
             real = grid[:outer, lane]
             imag = grid[outer:, lane]
-            rows.append(
-                jnp.concatenate(
-                    [
-                        real * real_twist - imag * imag_twist,
-                        real * imag_twist + imag * real_twist,
-                    ],
-                    axis=1,
-                )
-            )
-    return jnp.concatenate(rows, axis=0)
-
-
-def gather_back(spectrum, back_ref, twist_ref):
+            spun_real = real * real_twist - imag * imag_twist
+            spun_imag = real * imag_twist + imag * real_twist
+            far_real, far_imag = turn(spun_real), turn(spun_imag)
+            low = in_low(spun_real)
+            evens.append(jnp.where(low, spun_real + far_real, spun_imag + far_imag))
+            odds.append(jnp.where(low, spun_real - far_real, far_imag - spun_imag))
+    return jnp.concatenate(evens, axis=0), jnp.concatenate(odds, axis=0)
+
+
+def gather_back(even, odd, back_ref, twist_ref):
     real_twist = twist_ref[:, :LANES]
     imag_twist = twist_ref[:, LANES:]
     outer = real_twist.shape[0]
-    count = spectrum.shape[0] // outer
+    count = even.shape[0] // outer
     turned = []
     for which in range(count):
-        real = spectrum[which * outer : (which + 1) * outer, :LANES]
-        imag = spectrum[which * outer : (which + 1) * outer, LANES:]
+        rows = slice(which * outer, (which + 1) * outer)
+        total, change = even[rows] + odd[rows], even[rows] - odd[rows]
+        low = in_low(total)
+        real = jnp.where(low, total, turn(change))
+        imag = jnp.where(low, turn(total), change)
         turned.append(
             jnp.concatenate(
                 [
-                    real * real_twist - imag * imag_twist,
-                    -(imag * real_twist + real * imag_twist),
+                    real * real_twist + imag * imag_twist,
+                    imag * real_twist - real * imag_twist,
                 ],
                 axis=0,
             )
@@ -174,7 +187,9 @@
             values_ref[pl.ds(which * GROUP + k, outer, stride=channels), :] for k in range(GROUP)
         ]
         bins = group_rows(which, outer)
-        out_ref[bins, :] = mm_wide(spread(columns, wide_ref, twist_ref, False), mix_ref)
+        even, odd = spread(columns, wide_ref, twist_ref, False)
+        out_ref[bins, :LANES] = mm_packed(even, mix_ref[0])
+        out_ref[bins, LANES:] = mm_packed(odd, mix_ref[1])
         copies += start_all([(out_ref.at[bins], out_hbm.at[bins])], sems, which)
     inputs_ref[...] = mm(token_picks(ids_ref[...], embed_ref.shape[0]), embed_ref[...]).astype(
         BF16
@@ -191,19 +206,20 @@
         columns = [
             values_ref[pl.ds(base + k, outer, stride=channels), :] for k in range(GROUP)
         ]
-        bins = mm_wide(spread(columns, exact_ref, twist_ref, True), mix_ref)
+        pieces = spread(columns, exact_ref, twist_ref, True)
+        bins = [mm_packed(piece, mix_ref[half]) for half, piece in enumerate(pieces)]
         arrivals[which].wait()
         filt = spectrum_ref[group_rows(which, outer), :]
-        real, imag = bins[:, :LANES], bins[:, LANES:]
-        filt_real, filt_imag = filt[:, :LANES], filt[:, LANES:]
-        product = jnp.concatenate(
-            [
-                real * filt_real - sign * (imag * filt_imag),
-                -(imag * filt_real + sign * (real * filt_imag)),
-            ],
-            axis=1,
-        )
-        result = gather_back(mm_wide(product, mix_ref), back_ref, twist_ref)
+        pieces = []
+        for half in range(2):
+            own = filt[:, half * LANES : (half + 1) * LANES]
+            far = turn(own)
+            low = in_low(own)
+            straight = jnp.where(low, own, far)
+            crossed = jnp.where(low, -sign * far, sign * own)
+            product = bins[half] * straight + turn(bins[half]) * crossed
+            pieces.append(mm_packed(product, mix_ref[2 + half]))
+        result = gather_back(*pieces, back_ref, twist_ref)
         for k in range(GROUP):
             values_ref[pl.ds(base + k, outer, stride=channels), :] = result[k]
 
@@ -260,8 +276,10 @@
         blocks = width // LANES // CHUNKS
         for block in range(chunk * blocks, (chunk + 1) * blocks):
             lane = slice(block * LANES, (block + 1) * LANES)
-            inputs = mm(picks, embed_ref[:, lane]).astype(BF16).astype(F32)
-            turned = (grad_ref[:, lane].astype(F32) * inputs).T
+            if block % 2 == 0:
+                pair = slice(block * LANES, (block + 2) * LANES)
+                upstream = grad_ref[:, pair].astype(F32) * mm(picks, embed_ref[:, pair])
+            turned = upstream[:, (block % 2) * LANES : (block % 2 + 1) * LANES].T
             part = weight_ref[:, lane].astype(F32)
             parts = swap_blocks([part[8 * g : 8 * g + 8] for g in range(HALVES)])
             for k, piece in enumerate(parts):

time: 96.2 us -> 95.2 us (0.990)
  Pallas kernels: 29.5 us -> 27.9 us
  waiting for transfers between devices: 33.1 us -> 34.1 us
    all_to_all x3, waiting for transfers between devices: 24.3 us -> 25.3 us  [exchange(): lax.all_to_all(values, 'seq', split_axis=0, concat_axis=0, tiled=True)]
  transfers between devices with their start and end apart: 7 -> 7, of which waited for: 5 -> 5; matrix products, arithmetic and copies ran while one was open for 2% -> 2% of each run, Pallas kernels for 15% -> 14%
where the time goes in v4:
time: 95.2 us; the launch traced here: 94.7 us
  waiting for transfers between devices  34.1 us (36%)
  Pallas kernels  27.9 us (29%)
  starting transfers between devices  26.8 us (28%)
  local copies, waits for them, and re-layouts  3.19 us (3%)
  other arithmetic  1.65 us (2%)
  between operations  0.99 us (1%)
    all_to_all x3, waiting for transfers between devices, exchange(): lax.all_to_all(values, 'seq', split_axis=0, concat_axis=0, tiled=True)  25.3 us
    all_to_all x3, starting transfers between devices, exchange(): lax.all_to_all(values, 'seq', split_axis=0, concat_axis=0, tiled=True)  25.2 us
    pallas_call x1, Pallas kernels, per_device(): call(backward_kernel, (shape((parts, 8, tokens), F32), shape((2 * parts,...  9.26 us
    ppermute x3, waiting for transfers between devices, swap(): lax.ppermute(values, 'dp', [(source, source ^ flip) for source in range(r...  8.84 us
    pallas_call x1, Pallas kernels, per_device(): call(forward_kernel, shape((parts, channels, tokens), BF16), 'aahhhhhh',...  8.75 us
    pallas_call x1, Pallas kernels, per_device(): call(send_kernel, shape((parts, SIDE + TAIL, tokens), BF16), 'vhhh', 'h',...  3.92 us
    unnamed x20, local copies, waits for them, and re-layouts  3.19 us
    pallas_call x1, Pallas kernels, per_device(): call(spectrum_kernel, (shape((rows, 2 * tokens), F32), shape((tokens, wid...  2.59 us
  transfers between devices with their start and end apart: 7, of which 5 were waited for; matrix products, arithmetic and copies ran while one was open for 2% of the time, Pallas kernels for 14%

profile of v4, /device:TPU:6, one launch (start us, length us, event | category | flops | bytes accessed | tf_op | source)
XLA Modules:
  0.0 94.7 jit_solution(5779776346989905399)
XLA Ops:
  0.6 0.0 copy-start
  0.7 0.0 copy-start.3
  0.7 0.0 copy-start.4
  0.7 0.0 copy-start.5
  0.7 3.9 %shard_map.147 = bf16[64,40,128]{2,1,0:T(8,128)(2,1)} custom-call(s32[1,128]{1,0:T(1,128)} %ids_ref.3, bf16[512,2048]{1,0:T(8,128)(2,1)} %embed_hbm.5, bf16[128,2048]{1,0:T(8,128)(2,1)} %bitcast.7, bf16[32,2048]{1,0:T(8,128)(2,1)} %weight_hbm.1), custom_call_target="tpu_custom_call" | custom-call | flops 268435456 | bytes 5242880 | tf_op jit(solution)/shard_map/pallas_call | solution.py:616
  4.6 13.4 %all-to-all-start = ((bf16[64,40,128]{2,1,0:T(8,128)(2,1)}), bf16[64,40,128]{2,1,0:T(8,128)(2,1)}, u32[]{:S(2)}, u32[]{:S(2)}) async-start(bf16[64,40,128]{2,1,0:T(8,128)(2,1)} %shard_map.147), calls=%async_computation | async-start | bytes 1310720 | tf_op jit(solution)/shard_map/all_to_all | solution.py:596
  18.1 1.2 %copy-done.2 = f32[32,8192]{1,0:T(8,128)S(1)} copy-done((f32[32,8192]{1,0:T(8,128)S(1)}, f32[32,8192]{1,0:T(8,128)}, u32[]{:S(2)}) %copy-start.2) | copy-done | bytes 1048600
  19.3 2.6 %shard_map.148 = (f32[2048,256]{1,0:T(8,128)S(1)}, bf16[128,2048]{1,0:T(8,128)(2,1)S(1)}) custom-call(f32[32,8192]{1,0:T(8,128)S(1)} %copy-done.2, bf16[128,192]{1,0:T(8,128)(2,1)S(1)} %copy-done.5, f32[64,256]{1,0:T(8,128)S(1)} %copy-done.4, bf16[4,256,256]{2,1,0:T(8,128)(2,1)S(1)} %copy-done.3, s32[1,128]{1,0:T(1,128)S(1)} %copy-done.1, ...), custom_call_target="tpu_custom_call" | custom-call | flops 5368709120 | bytes 3145728 | tf_op jit(solution)/shard_map/pallas_call | solution.py:632
  21.9 1.3 %copy-done.6 = f32[2048,256]{1,0:T(8,128)} copy-done((f32[2048,256]{1,0:T(8,128)}, f32[2048,256]{1,0:T(8,128)S(1)}, u32[]{:S(2)}) %copy-start.6) | copy-done | bytes 2097176
  23.2 16.2 %all-to-all-done.block_ref = bf16[64,40,128]{2,1,0:T(8,128)(2,1)} async-done(((bf16[64,40,128]{2,1,0:T(8,128)(2,1)}), bf16[64,40,128]{2,1,0:T(8,128)(2,1)}, u32[]{:S(2)}, u32[]{:S(2)}) %all-to-all-start) | async-done | bytes 655392 | tf_op jit(solution)/shard_map/all_to_all | solution.py:596
  39.4 9.3 %shard_map.149 = (f32[64,8,128]{2,1,0:T(8,128)}, bf16[128,128]{1,0:T(8,128)(2,1)}, bf16[512,128]{1,0:T(8,128)(2,1)}) custom-call(bf16[64,40,128]{2,1,0:T(8,128)(2,1)} %all-to-all-done.block_ref, bf16[512,2048]{1,0:T(8,128)(2,1)} %embed_hbm.5, f32[2048,256]{1,0:T(8,128)} %copy-done.6, bf16[128,128]{1,0:T(8,128)(2,1)} %constant.18.clone.exact_hbm, ...), custom_call_target="tpu_custom_call" | custom-call | flops 10737418240 | bytes 6291456 | tf_op jit(solution)/shard_map/pallas_call | solution.py:646
  48.7 0.1 collective-permute-start
  48.8 5.1 %all-to-all-start.2 = ((f32[64,8,128]{2,1,0:T(8,128)}), f32[64,8,128]{2,1,0:T(8,128)S(1)}, u32[]{:S(2)}, u32[]{:S(2)}) async-start(f32[64,8,128]{2,1,0:T(8,128)} %get-tuple-element.16), calls=%async_computation.2 | async-start | bytes 524288 | tf_op jit(solution)/shard_map/all_to_all | solution.py:596
  53.9 0.6 copy-done.9
  54.5 8.7 %shard_map.150 = bf16[64,32,128]{2,1,0:T(8,128)(2,1)} custom-call(bf16[512,128]{1,0:T(8,128)(2,1)} %get-tuple-element.13.tails_hbm, bf16[128,128]{1,0:T(8,128)(2,1)} %copy-done.9, bf16[512,2048]{1,0:T(8,128)(2,1)} %embed_hbm.5, f32[2048,256]{1,0:T(8,128)} %copy-done.6, bf16[128,128]{1,0:T(8,128)(2,1)} %constant.18.clone.exact_hbm, ...), custom_call_target="tpu_custom_call" | custom-call | flops 10737418240 | bytes 6291456 | tf_op jit(solution)/shard_map/pallas_call | solution.py:672
  63.3 4.6 %all-to-all-done.2.grad_hbm = f32[64,8,128]{2,1,0:T(8,128)S(1)} async-done(((f32[64,8,128]{2,1,0:T(8,128)}), f32[64,8,128]{2,1,0:T(8,128)S(1)}, u32[]{:S(2)}, u32[]{:S(2)}) %all-to-all-start.2) | async-done | bytes 262176 | tf_op jit(solution)/shard_map/all_to_all | solution.py:596
  67.9 6.8 %all-to-all-start.1 = ((bf16[64,32,128]{2,1,0:T(8,128)(2,1)}), bf16[64,32,128]{2,1,0:T(8,128)(2,1)S(1)}, u32[]{:S(2)}, u32[]{:S(2)}) async-start(bf16[64,32,128]{2,1,0:T(8,128)(2,1)} %shard_map.150), calls=%async_computation.1 | async-start | bytes 1048576 | tf_op jit(solution)/shard_map/all_to_all | solution.py:596
  74.6 2.4 %shard_map.152 = (f32[32,2048]{1,0:T(8,128)}, f32[32,2048]{1,0:T(8,128)}, bf16[32,2048]{1,0:T(8,128)(2,1)}) custom-call(f32[64,8,128]{2,1,0:T(8,128)} %copy-done.7, f32[32,2048]{1,0:T(8,128)} %bitcast.8, f32[32,2048]{1,0:T(8,128)} %bitcast.9), custom_call_target="tpu_custom_call" | custom-call | flops 1048576 | bytes 2097152 | tf_op jit(solution)/shard_map/pallas_call | solution.py:694
  77.0 1.5 %collective-permute-start.2 = (bf16[32,2048]{1,0:T(8,128)(2,1)}, bf16[32,2048]{1,0:T(8,128)(2,1)S(1)}, u32[]{:S(2)}, u32[]{:S(2)}) collective-permute-start(bf16[32,2048]{1,0:T(8,128)(2,1)} %get-tuple-element.19), channel_id=1, source_target_pairs={{0,128},{64,192},{128,0},{192,64},{1,129},{65,193},{129,1},{193,65... | collective-permute-start | bytes 393224 | tf_op jit(solution)/shard_map/ppermute | solution.py:715
  78.5 7.5 %collective-permute-done.2 = bf16[32,2048]{1,0:T(8,128)(2,1)S(1)} collective-permute-done((bf16[32,2048]{1,0:T(8,128)(2,1)}, bf16[32,2048]{1,0:T(8,128)(2,1)S(1)}, u32[]{:S(2)}, u32[]{:S(2)}) %collective-permute-start.2) | collective-permute-done | bytes 131104 | tf_op jit(solution)/shard_map/ppermute | solution.py:715
  86.0 1.3 %collective-permute-done.3 = bf16[32,2048]{1,0:T(8,128)(2,1)S(1)} collective-permute-done((bf16[32,2048]{1,0:T(8,128)(2,1)S(1)}, bf16[32,2048]{1,0:T(8,128)(2,1)S(1)}, u32[]{:S(2)}, u32[]{:S(2)}) %collective-permute-start.3) | collective-permute-done | bytes 131104 | tf_op jit(solution)/shard_map/ppermute | solution.py:715
  87.3 1.7 %subtract_convert_fusion = bf16[32,2048]{1,0:T(8,128)(2,1)} fusion(bf16[32,2048]{1,0:T(8,128)(2,1)S(1)} %collective-permute-done.3, bf16[32,2048]{1,0:T(8,128)(2,1)S(1)} %collective-permute-done.2, bf16[32,2048]{1,0:T(8,128)(2,1)S(1)} %collective-permute-done.1, bf16[32,2048]{1,0:T(8,128)(2,1)} %get-tuple-element.19, bf16[32,2048]{1,0:T(8,128)(2,1)S(1)} %copy-done.8), kind=kLoop, calls=%fused_computation | loop fusion | flops 720896 | bytes 786432 | tf_op jit(solution)/shard_map/convert_element_type | solution.py:723
  89.0 4.5 %all-to-all-done.1.conv_ref = bf16[64,32,128]{2,1,0:T(8,128)(2,1)S(1)} async-done(((bf16[64,32,128]{2,1,0:T(8,128)(2,1)}), bf16[64,32,128]{2,1,0:T(8,128)(2,1)S(1)}, u32[]{:S(2)}, u32[]{:S(2)}) %all-to-all-start.1) | async-done | bytes 524320 | tf_op jit(solution)/shard_map/all_to_all | solution.py:596
  93.5 1.1 %shard_map.151 = bf16[128,2048]{1,0:T(8,128)(2,1)} custom-call(bf16[64,32,128]{2,1,0:T(8,128)(2,1)S(1)} %all-to-all-done.1.conv_ref, bf16[128,2048]{1,0:T(8,128)(2,1)S(1)} %get-tuple-element.15.inputs_hbm), custom_call_target="tpu_custom_call" | custom-call | flops 1048576 | bytes 2097152 | tf_op jit(solution)/shard_map/pallas_call | solution.py:724
  (17 shorter events, 0.0 us)
Async XLA Ops:
  0.6 17.4 %copy-start = (bf16[512,2048]{1,0:T(8,128)(2,1)S(1)}, bf16[512,2048]{1,0:T(8,128)(2,1)}, u32[]{:S(2)}) copy-start(bf16[512,2048]{1,0:T(8,128)(2,1)} %embed_hbm.5) | copy-start | bytes 6291460
  0.6 17.4 %copy-start.1 = (s32[1,128]{1,0:T(1,128)S(1)}, s32[1,128]{1,0:T(1,128)}, u32[]{:S(2)}) copy-start(s32[1,128]{1,0:T(1,128)} %ids_ref.3) | copy-start | bytes 1540
  0.7 17.4 %copy-start.3 = (bf16[4,256,256]{2,1,0:T(8,128)(2,1)S(1)}, bf16[4,256,256]{2,1,0:T(8,128)(2,1)}, u32[]{:S(2)}) copy-start(bf16[4,256,256]{2,1,0:T(8,128)(2,1)} %constant.17.clone.mix_ref.mix_hbm) | copy-start | bytes 1572868
  0.7 17.4 %copy-start.4 = (f32[64,256]{1,0:T(8,128)S(1)}, f32[64,256]{1,0:T(8,128)}, u32[]{:S(2)}) copy-start(f32[64,256]{1,0:T(8,128)} %constant.16.clone.twist_ref.twist_hbm) | copy-start | bytes 196612
  0.7 17.4 %copy-start.5 = (bf16[128,192]{1,0:T(8,128)(2,1)S(1)}, bf16[128,192]{1,0:T(8,128)(2,1)}, u32[]{:S(2)}) copy-start(bf16[128,192]{1,0:T(8,128)(2,1)} %constant.15.clone.wide_ref) | copy-start | bytes 147460
  4.6 34.8 %all-to-all-start = ((bf16[64,40,128]{2,1,0:T(8,128)(2,1)}), bf16[64,40,128]{2,1,0:T(8,128)(2,1)}, u32[]{:S(2)}, u32[]{:S(2)}) async-start(bf16[64,40,128]{2,1,0:T(8,128)(2,1)} %shard_map.147), calls=%async_computation | async-start | bytes 1310720 | tf_op jit(solution)/shard_map/all_to_all | solution.py:596
  18.1 1.2 %copy-start.2 = (f32[32,8192]{1,0:T(8,128)S(1)}, f32[32,8192]{1,0:T(8,128)}, u32[]{:S(2)}) copy-start(f32[32,8192]{1,0:T(8,128)} %filters_ref.1) | copy-start | bytes 3145732
  21.9 1.3 %copy-start.6 = (f32[2048,256]{1,0:T(8,128)}, f32[2048,256]{1,0:T(8,128)S(1)}, u32[]{:S(2)}) copy-start(f32[2048,256]{1,0:T(8,128)S(1)} %get-tuple-element.12.spectrum_hbm) | copy-start | bytes 6291460
  48.7 5.2 %collective-permute-start = (bf16[128,128]{1,0:T(8,128)(2,1)}, bf16[128,128]{1,0:T(8,128)(2,1)S(1)}, u32[]{:S(2)}, u32[]{:S(2)}) collective-permute-start(bf16[128,128]{1,0:T(8,128)(2,1)} %get-tuple-element.14), channel_id=1, source_target_pairs={{0,64},{64,0},{128,192},{192,128},{1,65},{65,1},{129,193},{193,129... | collective-permute-start | bytes 98312 | tf_op jit(solution)/shard_map/ppermute | solution.py:670
  48.8 19.0 %all-to-all-start.2 = ((f32[64,8,128]{2,1,0:T(8,128)}), f32[64,8,128]{2,1,0:T(8,128)S(1)}, u32[]{:S(2)}, u32[]{:S(2)}) async-start(f32[64,8,128]{2,1,0:T(8,128)} %get-tuple-element.16), calls=%async_computation.2 | async-start | bytes 524288 | tf_op jit(solution)/shard_map/all_to_all | solution.py:596
  53.9 0.6 copy-start.9
  54.5 32.8 %copy-start.8 = (bf16[32,2048]{1,0:T(8,128)(2,1)S(1)}, bf16[32,2048]{1,0:T(8,128)(2,1)}, u32[]{:S(2)}) copy-start(bf16[32,2048]{1,0:T(8,128)(2,1)} %weight_hbm.1) | copy-start | bytes 393220
  67.9 6.8 %copy-start.7 = (f32[64,8,128]{2,1,0:T(8,128)}, f32[64,8,128]{2,1,0:T(8,128)S(1)}, u32[]{:S(2)}) copy-start(f32[64,8,128]{2,1,0:T(8,128)S(1)} %all-to-all-done.2.grad_hbm) | copy-start | bytes 786436
  67.9 25.6 %all-to-all-start.1 = ((bf16[64,32,128]{2,1,0:T(8,128)(2,1)}), bf16[64,32,128]{2,1,0:T(8,128)(2,1)S(1)}, u32[]{:S(2)}, u32[]{:S(2)}) async-start(bf16[64,32,128]{2,1,0:T(8,128)(2,1)} %shard_map.150), calls=%async_computation.1 | async-start | bytes 1048576 | tf_op jit(solution)/shard_map/all_to_all | solution.py:596
  77.0 9.0 %collective-permute-start.2 = (bf16[32,2048]{1,0:T(8,128)(2,1)}, bf16[32,2048]{1,0:T(8,128)(2,1)S(1)}, u32[]{:S(2)}, u32[]{:S(2)}) collective-permute-start(bf16[32,2048]{1,0:T(8,128)(2,1)} %get-tuple-element.19), channel_id=1, source_target_pairs={{0,128},{64,192},{128,0},{192,64},{1,129},{65,193},{129,1},{193,65... | collective-permute-start | bytes 393224 | tf_op jit(solution)/shard_map/ppermute | solution.py:715
  78.5 7.5 %collective-permute-start.1 = (bf16[32,2048]{1,0:T(8,128)(2,1)}, bf16[32,2048]{1,0:T(8,128)(2,1)S(1)}, u32[]{:S(2)}, u32[]{:S(2)}) collective-permute-start(bf16[32,2048]{1,0:T(8,128)(2,1)} %get-tuple-element.19), channel_id=1, source_target_pairs={{0,64},{64,0},{128,192},{192,128},{1,65},{65,1},{129,193},{193,129... | collective-permute-start | bytes 393224 | tf_op jit(solution)/shard_map/ppermute | solution.py:715
  86.0 1.3 %collective-permute-start.3 = (bf16[32,2048]{1,0:T(8,128)(2,1)S(1)}, bf16[32,2048]{1,0:T(8,128)(2,1)S(1)}, u32[]{:S(2)}, u32[]{:S(2)}) collective-permute-start(bf16[32,2048]{1,0:T(8,128)(2,1)S(1)} %collective-permute-done.2), channel_id=1, source_target_pairs={{0,64},{64,0},{128,192},{192,128},{1,65},{65,1},{129,193},{193,129... | collective-permute-start | bytes 393224 | tf_op jit(solution)/shard_map/ppermute | solution.py:715

commit v5 on v4

--- a/solution.py
+++ b/solution.py
@@ -16,7 +16,7 @@
 F32 = jnp.float32
 BF16 = jnp.bfloat16
 LANES = 128
-GROUP = 32
+GROUP = 16
 STEP = 32
 TAIL = 8
 SENT = 6
@@ -468,10 +468,13 @@
             first = step * STEP + k
             high, picks = read_ids(tails_ref, first)
             rows = values_ref[pl.ds(pl.multiple_of(first * SIDE, 2 * SIDE), 2 * SIDE), :]
-            columns = jnp.concatenate([rows[:SIDE], rows[SIDE:]], axis=1)
-            masked = [jnp.where(high == part, columns, 0.0) for part in range(vocab // LANES)]
+            columns = jnp.concatenate([rows[:SIDE], rows[SIDE:]], axis=1).astype(BF16)
+            masked = [
+                columns * jnp.where(high == part, 1.0, 0.0).astype(BF16)
+                for part in range(vocab // LANES)
+            ]
             total = total + lax.dot_general(
-                jnp.concatenate(masked, axis=0).astype(BF16),
+                jnp.concatenate(masked, axis=0),
                 picks,
                 (((1,), (1,)), ((), ())),
                 preferred_element_type=F32,

time: 95.2 us -> 94.8 us (level)
  no operation moved by 1% of the time
where the time goes in v5:
time: 94.8 us; the launch traced here: 94.4 us
  waiting for transfers between devices  34.3 us (36%)
  Pallas kernels  27.5 us (29%)
  starting transfers between devices  26.7 us (28%)
  local copies, waits for them, and re-layouts  3.19 us (3%)
  other arithmetic  1.65 us (2%)
  between operations  0.99 us (1%)
    all_to_all x3, waiting for transfers between devices, exchange(): lax.all_to_all(values, 'seq', split_axis=0, concat_axis=0, tiled=True)  25.5 us
    all_to_all x3, starting transfers between devices, exchange(): lax.all_to_all(values, 'seq', split_axis=0, concat_axis=0, tiled=True)  25.1 us
    pallas_call x1, Pallas kernels, per_device(): call(backward_kernel, (shape((parts, 8, tokens), F32), shape((2 * parts,...  9.06 us
    ppermute x3, waiting for transfers between devices, swap(): lax.ppermute(values, 'dp', [(source, source ^ flip) for source in range(r...  8.85 us
    pallas_call x1, Pallas kernels, per_device(): call(forward_kernel, shape((parts, channels, tokens), BF16), 'aahhhhhh',...  8.61 us
    pallas_call x1, Pallas kernels, per_device(): call(send_kernel, shape((parts, SIDE + TAIL, tokens), BF16), 'vhhh', 'h',...  3.92 us
    unnamed x20, local copies, waits for them, and re-layouts  3.19 us
    pallas_call x1, Pallas kernels, per_device(): call(spectrum_kernel, (shape((rows, 2 * tokens), F32), shape((tokens, wid...  2.51 us
  transfers between devices with their start and end apart: 7, of which 5 were waited for; matrix products, arithmetic and copies ran while one was open for 2% of the time, Pallas kernels for 14%

profile of v5, /device:TPU:6, one launch (start us, length us, event | category | flops | bytes accessed | tf_op | source)
XLA Modules:
  0.0 94.4 jit_solution(12858359727272827355)
XLA Ops:
  0.6 0.0 copy-start
  0.7 0.0 copy-start.3
  0.7 0.0 copy-start.4
  0.7 0.0 copy-start.5
  0.7 3.9 %shard_map.147 = bf16[64,40,128]{2,1,0:T(8,128)(2,1)} custom-call(s32[1,128]{1,0:T(1,128)} %ids_ref.3, bf16[512,2048]{1,0:T(8,128)(2,1)} %embed_hbm.5, bf16[128,2048]{1,0:T(8,128)(2,1)} %bitcast.7, bf16[32,2048]{1,0:T(8,128)(2,1)} %weight_hbm.1), custom_call_target="tpu_custom_call" | custom-call | flops 268435456 | bytes 5242880 | tf_op jit(solution)/shard_map/pallas_call | solution.py:619
  4.6 13.4 %all-to-all-start = ((bf16[64,40,128]{2,1,0:T(8,128)(2,1)}), bf16[64,40,128]{2,1,0:T(8,128)(2,1)}, u32[]{:S(2)}, u32[]{:S(2)}) async-start(bf16[64,40,128]{2,1,0:T(8,128)(2,1)} %shard_map.147), calls=%async_computation | async-start | bytes 1310720 | tf_op jit(solution)/shard_map/all_to_all | solution.py:599
  18.1 1.2 %copy-done.2 = f32[32,8192]{1,0:T(8,128)S(1)} copy-done((f32[32,8192]{1,0:T(8,128)S(1)}, f32[32,8192]{1,0:T(8,128)}, u32[]{:S(2)}) %copy-start.2) | copy-done | bytes 1048600
  19.3 2.5 %shard_map.148 = (f32[2048,256]{1,0:T(8,128)S(1)}, bf16[128,2048]{1,0:T(8,128)(2,1)S(1)}) custom-call(f32[32,8192]{1,0:T(8,128)S(1)} %copy-done.2, bf16[128,192]{1,0:T(8,128)(2,1)S(1)} %copy-done.5, f32[64,256]{1,0:T(8,128)S(1)} %copy-done.4, bf16[4,256,256]{2,1,0:T(8,128)(2,1)S(1)} %copy-done.3, s32[1,128]{1,0:T(1,128)S(1)} %copy-done.1, ...), custom_call_target="tpu_custom_call" | custom-call | flops 5368709120 | bytes 3145728 | tf_op jit(solution)/shard_map/pallas_call | solution.py:635
  21.8 1.3 %copy-done.6 = f32[2048,256]{1,0:T(8,128)} copy-done((f32[2048,256]{1,0:T(8,128)}, f32[2048,256]{1,0:T(8,128)S(1)}, u32[]{:S(2)}) %copy-start.6) | copy-done | bytes 2097176
  23.1 16.3 %all-to-all-done.block_ref = bf16[64,40,128]{2,1,0:T(8,128)(2,1)} async-done(((bf16[64,40,128]{2,1,0:T(8,128)(2,1)}), bf16[64,40,128]{2,1,0:T(8,128)(2,1)}, u32[]{:S(2)}, u32[]{:S(2)}) %all-to-all-start) | async-done | bytes 655392 | tf_op jit(solution)/shard_map/all_to_all | solution.py:599
  39.4 9.1 %shard_map.149 = (f32[64,8,128]{2,1,0:T(8,128)}, bf16[128,128]{1,0:T(8,128)(2,1)}, bf16[512,128]{1,0:T(8,128)(2,1)}) custom-call(bf16[64,40,128]{2,1,0:T(8,128)(2,1)} %all-to-all-done.block_ref, bf16[512,2048]{1,0:T(8,128)(2,1)} %embed_hbm.5, f32[2048,256]{1,0:T(8,128)} %copy-done.6, bf16[128,128]{1,0:T(8,128)(2,1)} %constant.18.clone.exact_hbm, ...), custom_call_target="tpu_custom_call" | custom-call | flops 10737418240 | bytes 6291456 | tf_op jit(solution)/shard_map/pallas_call | solution.py:649
  48.5 0.1 collective-permute-start
  48.6 5.1 %all-to-all-start.2 = ((f32[64,8,128]{2,1,0:T(8,128)}), f32[64,8,128]{2,1,0:T(8,128)S(1)}, u32[]{:S(2)}, u32[]{:S(2)}) async-start(f32[64,8,128]{2,1,0:T(8,128)} %get-tuple-element.16), calls=%async_computation.2 | async-start | bytes 524288 | tf_op jit(solution)/shard_map/all_to_all | solution.py:599
  53.7 0.6 copy-done.9
  54.3 8.6 %shard_map.150 = bf16[64,32,128]{2,1,0:T(8,128)(2,1)} custom-call(bf16[512,128]{1,0:T(8,128)(2,1)} %get-tuple-element.13.tails_hbm, bf16[128,128]{1,0:T(8,128)(2,1)} %copy-done.9, bf16[512,2048]{1,0:T(8,128)(2,1)} %embed_hbm.5, f32[2048,256]{1,0:T(8,128)} %copy-done.6, bf16[128,128]{1,0:T(8,128)(2,1)} %constant.18.clone.exact_hbm, ...), custom_call_target="tpu_custom_call" | custom-call | flops 10737418240 | bytes 6291456 | tf_op jit(solution)/shard_map/pallas_call | solution.py:675
  62.9 4.7 %all-to-all-done.2.grad_hbm = f32[64,8,128]{2,1,0:T(8,128)S(1)} async-done(((f32[64,8,128]{2,1,0:T(8,128)}), f32[64,8,128]{2,1,0:T(8,128)S(1)}, u32[]{:S(2)}, u32[]{:S(2)}) %all-to-all-start.2) | async-done | bytes 262176 | tf_op jit(solution)/shard_map/all_to_all | solution.py:599
  67.7 6.6 %all-to-all-start.1 = ((bf16[64,32,128]{2,1,0:T(8,128)(2,1)}), bf16[64,32,128]{2,1,0:T(8,128)(2,1)S(1)}, u32[]{:S(2)}, u32[]{:S(2)}) async-start(bf16[64,32,128]{2,1,0:T(8,128)(2,1)} %shard_map.150), calls=%async_computation.1 | async-start | bytes 1048576 | tf_op jit(solution)/shard_map/all_to_all | solution.py:599
  74.3 2.4 %shard_map.152 = (f32[32,2048]{1,0:T(8,128)}, f32[32,2048]{1,0:T(8,128)}, bf16[32,2048]{1,0:T(8,128)(2,1)}) custom-call(f32[64,8,128]{2,1,0:T(8,128)} %copy-done.7, f32[32,2048]{1,0:T(8,128)} %bitcast.8, f32[32,2048]{1,0:T(8,128)} %bitcast.9), custom_call_target="tpu_custom_call" | custom-call | flops 1048576 | bytes 2097152 | tf_op jit(solution)/shard_map/pallas_call | solution.py:697
  76.7 1.5 %collective-permute-start.2 = (bf16[32,2048]{1,0:T(8,128)(2,1)}, bf16[32,2048]{1,0:T(8,128)(2,1)S(1)}, u32[]{:S(2)}, u32[]{:S(2)}) collective-permute-start(bf16[32,2048]{1,0:T(8,128)(2,1)} %get-tuple-element.19), channel_id=1, source_target_pairs={{0,128},{64,192},{128,0},{192,64},{1,129},{65,193},{129,1},{193,65... | collective-permute-start | bytes 393224 | tf_op jit(solution)/shard_map/ppermute | solution.py:718
  78.1 7.5 %collective-permute-done.2 = bf16[32,2048]{1,0:T(8,128)(2,1)S(1)} collective-permute-done((bf16[32,2048]{1,0:T(8,128)(2,1)}, bf16[32,2048]{1,0:T(8,128)(2,1)S(1)}, u32[]{:S(2)}, u32[]{:S(2)}) %collective-permute-start.2) | collective-permute-done | bytes 131104 | tf_op jit(solution)/shard_map/ppermute | solution.py:718
  85.7 1.3 %collective-permute-done.3 = bf16[32,2048]{1,0:T(8,128)(2,1)S(1)} collective-permute-done((bf16[32,2048]{1,0:T(8,128)(2,1)S(1)}, bf16[32,2048]{1,0:T(8,128)(2,1)S(1)}, u32[]{:S(2)}, u32[]{:S(2)}) %collective-permute-start.3) | collective-permute-done | bytes 131104 | tf_op jit(solution)/shard_map/ppermute | solution.py:718
  87.0 1.7 %subtract_convert_fusion = bf16[32,2048]{1,0:T(8,128)(2,1)} fusion(bf16[32,2048]{1,0:T(8,128)(2,1)S(1)} %collective-permute-done.3, bf16[32,2048]{1,0:T(8,128)(2,1)S(1)} %collective-permute-done.2, bf16[32,2048]{1,0:T(8,128)(2,1)S(1)} %collective-permute-done.1, bf16[32,2048]{1,0:T(8,128)(2,1)} %get-tuple-element.19, bf16[32,2048]{1,0:T(8,128)(2,1)S(1)} %copy-done.8), kind=kLoop, calls=%fused_computation | loop fusion | flops 720896 | bytes 786432 | tf_op jit(solution)/shard_map/convert_element_type | solution.py:726
  88.7 4.5 %all-to-all-done.1.conv_ref = bf16[64,32,128]{2,1,0:T(8,128)(2,1)S(1)} async-done(((bf16[64,32,128]{2,1,0:T(8,128)(2,1)}), bf16[64,32,128]{2,1,0:T(8,128)(2,1)S(1)}, u32[]{:S(2)}, u32[]{:S(2)}) %all-to-all-start.1) | async-done | bytes 524320 | tf_op jit(solution)/shard_map/all_to_all | solution.py:599
  93.1 1.1 %shard_map.151 = bf16[128,2048]{1,0:T(8,128)(2,1)} custom-call(bf16[64,32,128]{2,1,0:T(8,128)(2,1)S(1)} %all-to-all-done.1.conv_ref, bf16[128,2048]{1,0:T(8,128)(2,1)S(1)} %get-tuple-element.15.inputs_hbm), custom_call_target="tpu_custom_call" | custom-call | flops 1048576 | bytes 2097152 | tf_op jit(solution)/shard_map/pallas_call | solution.py:727
  (17 shorter events, 0.0 us)
Async XLA Ops:
  0.6 17.4 %copy-start = (bf16[512,2048]{1,0:T(8,128)(2,1)S(1)}, bf16[512,2048]{1,0:T(8,128)(2,1)}, u32[]{:S(2)}) copy-start(bf16[512,2048]{1,0:T(8,128)(2,1)} %embed_hbm.5) | copy-start | bytes 6291460
  0.6 17.4 %copy-start.1 = (s32[1,128]{1,0:T(1,128)S(1)}, s32[1,128]{1,0:T(1,128)}, u32[]{:S(2)}) copy-start(s32[1,128]{1,0:T(1,128)} %ids_ref.3) | copy-start | bytes 1540
  0.7 17.4 %copy-start.3 = (bf16[4,256,256]{2,1,0:T(8,128)(2,1)S(1)}, bf16[4,256,256]{2,1,0:T(8,128)(2,1)}, u32[]{:S(2)}) copy-start(bf16[4,256,256]{2,1,0:T(8,128)(2,1)} %constant.17.clone.mix_ref.mix_hbm) | copy-start | bytes 1572868
  0.7 17.4 %copy-start.4 = (f32[64,256]{1,0:T(8,128)S(1)}, f32[64,256]{1,0:T(8,128)}, u32[]{:S(2)}) copy-start(f32[64,256]{1,0:T(8,128)} %constant.16.clone.twist_ref.twist_hbm) | copy-start | bytes 196612
  0.7 17.4 %copy-start.5 = (bf16[128,192]{1,0:T(8,128)(2,1)S(1)}, bf16[128,192]{1,0:T(8,128)(2,1)}, u32[]{:S(2)}) copy-start(bf16[128,192]{1,0:T(8,128)(2,1)} %constant.15.clone.wide_ref) | copy-start | bytes 147460
  4.6 34.8 %all-to-all-start = ((bf16[64,40,128]{2,1,0:T(8,128)(2,1)}), bf16[64,40,128]{2,1,0:T(8,128)(2,1)}, u32[]{:S(2)}, u32[]{:S(2)}) async-start(bf16[64,40,128]{2,1,0:T(8,128)(2,1)} %shard_map.147), calls=%async_computation | async-start | bytes 1310720 | tf_op jit(solution)/shard_map/all_to_all | solution.py:599
  18.1 1.2 %copy-start.2 = (f32[32,8192]{1,0:T(8,128)S(1)}, f32[32,8192]{1,0:T(8,128)}, u32[]{:S(2)}) copy-start(f32[32,8192]{1,0:T(8,128)} %filters_ref.1) | copy-start | bytes 3145732
  21.8 1.3 %copy-start.6 = (f32[2048,256]{1,0:T(8,128)}, f32[2048,256]{1,0:T(8,128)S(1)}, u32[]{:S(2)}) copy-start(f32[2048,256]{1,0:T(8,128)S(1)} %get-tuple-element.12.spectrum_hbm) | copy-start | bytes 6291460
  48.5 5.2 %collective-permute-start = (bf16[128,128]{1,0:T(8,128)(2,1)}, bf16[128,128]{1,0:T(8,128)(2,1)S(1)}, u32[]{:S(2)}, u32[]{:S(2)}) collective-permute-start(bf16[128,128]{1,0:T(8,128)(2,1)} %get-tuple-element.14), channel_id=1, source_target_pairs={{0,64},{64,0},{128,192},{192,128},{1,65},{65,1},{129,193},{193,129... | collective-permute-start | bytes 98312 | tf_op jit(solution)/shard_map/ppermute | solution.py:673
  48.6 19.0 %all-to-all-start.2 = ((f32[64,8,128]{2,1,0:T(8,128)}), f32[64,8,128]{2,1,0:T(8,128)S(1)}, u32[]{:S(2)}, u32[]{:S(2)}) async-start(f32[64,8,128]{2,1,0:T(8,128)} %get-tuple-element.16), calls=%async_computation.2 | async-start | bytes 524288 | tf_op jit(solution)/shard_map/all_to_all | solution.py:599
  53.7 0.6 copy-start.9
  54.3 32.7 %copy-start.8 = (bf16[32,2048]{1,0:T(8,128)(2,1)S(1)}, bf16[32,2048]{1,0:T(8,128)(2,1)}, u32[]{:S(2)}) copy-start(bf16[32,2048]{1,0:T(8,128)(2,1)} %weight_hbm.1) | copy-start | bytes 393220
  67.7 6.6 %copy-start.7 = (f32[64,8,128]{2,1,0:T(8,128)}, f32[64,8,128]{2,1,0:T(8,128)S(1)}, u32[]{:S(2)}) copy-start(f32[64,8,128]{2,1,0:T(8,128)S(1)} %all-to-all-done.2.grad_hbm) | copy-start | bytes 786436
  67.7 25.5 %all-to-all-start.1 = ((bf16[64,32,128]{2,1,0:T(8,128)(2,1)}), bf16[64,32,128]{2,1,0:T(8,128)(2,1)S(1)}, u32[]{:S(2)}, u32[]{:S(2)}) async-start(bf16[64,32,128]{2,1,0:T(8,128)(2,1)} %shard_map.150), calls=%async_computation.1 | async-start | bytes 1048576 | tf_op jit(solution)/shard_map/all_to_all | solution.py:599
  76.7 9.0 %collective-permute-start.2 = (bf16[32,2048]{1,0:T(8,128)(2,1)}, bf16[32,2048]{1,0:T(8,128)(2,1)S(1)}, u32[]{:S(2)}, u32[]{:S(2)}) collective-permute-start(bf16[32,2048]{1,0:T(8,128)(2,1)} %get-tuple-element.19), channel_id=1, source_target_pairs={{0,128},{64,192},{128,0},{192,64},{1,129},{65,193},{129,1},{193,65... | collective-permute-start | bytes 393224 | tf_op jit(solution)/shard_map/ppermute | solution.py:718
  78.1 7.5 %collective-permute-start.1 = (bf16[32,2048]{1,0:T(8,128)(2,1)}, bf16[32,2048]{1,0:T(8,128)(2,1)S(1)}, u32[]{:S(2)}, u32[]{:S(2)}) collective-permute-start(bf16[32,2048]{1,0:T(8,128)(2,1)} %get-tuple-element.19), channel_id=1, source_target_pairs={{0,64},{64,0},{128,192},{192,128},{1,65},{65,1},{129,193},{193,129... | collective-permute-start | bytes 393224 | tf_op jit(solution)/shard_map/ppermute | solution.py:718
  85.6 1.3 %collective-permute-start.3 = (bf16[32,2048]{1,0:T(8,128)(2,1)S(1)}, bf16[32,2048]{1,0:T(8,128)(2,1)S(1)}, u32[]{:S(2)}, u32[]{:S(2)}) collective-permute-start(bf16[32,2048]{1,0:T(8,128)(2,1)S(1)} %collective-permute-done.2), channel_id=1, source_target_pairs={{0,64},{64,0},{128,192},{192,128},{1,65},{65,1},{129,193},{193,129... | collective-permute-start | bytes 393224 | tf_op jit(solution)/shard_map/ppermute | solution.py:718

commit v6 on v5

--- a/solution.py
+++ b/solution.py
@@ -712,7 +712,7 @@
         ],
         flops=1 << 20,
         moved=2 << 20,
-        limit=60817408,
+        limit=16777216,
     )(gradient, momentum[0], feedback[0])
     def swap(values, flip):
         return lax.ppermute(values, "dp", [(source, source ^ flip) for source in range(replicas)])

time: 94.8 us -> 94.8 us (level)
  waiting for transfers between devices: 34.3 us -> 35.8 us
    all_to_all x3, waiting for transfers between devices: 25.5 us -> 27.7 us  [exchange(): lax.all_to_all(values, 'seq', split_axis=0, concat_axis=0, tiled=True)]
    unnamed x20 -> x22, local copies, waits for them, and re-layouts: 3.19 us -> 3.19 us
  transfers between devices with their start and end apart: 7 -> 7, of which waited for: 5 -> 5; matrix products, arithmetic and copies ran while one was open for 2% -> 1% of each run, Pallas kernels for 14% -> 14%
where the time goes in v6:
time: 94.8 us; the launch traced here: 94.4 us
  waiting for transfers between devices  35.8 us (38%)
  Pallas kernels  27 us (28%)
  starting transfers between devices  26.7 us (28%)
  local copies, waits for them, and re-layouts  3.19 us (3%)
  between operations  1 us (1%)
    all_to_all x3, waiting for transfers between devices, exchange(): lax.all_to_all(values, 'seq', split_axis=0, concat_axis=0, tiled=True)  27.7 us
    all_to_all x3, starting transfers between devices, exchange(): lax.all_to_all(values, 'seq', split_axis=0, concat_axis=0, tiled=True)  25.1 us
    pallas_call x1, Pallas kernels, per_device(): call(backward_kernel, (shape((parts, 8, tokens), F32), shape((2 * parts,...  9.06 us
    pallas_call x1, Pallas kernels, per_device(): call(forward_kernel, shape((parts, channels, tokens), BF16), 'aahhhhhh',...  8.64 us
    ppermute x3, waiting for transfers between devices, swap(): lax.ppermute(values, 'dp', [(source, source ^ flip) for source in range(r...  8.1 us
    pallas_call x1, Pallas kernels, per_device(): call(send_kernel, shape((parts, SIDE + TAIL, tokens), BF16), 'vhhh', 'h',...  3.9 us
    unnamed x22, local copies, waits for them, and re-layouts  3.19 us
    pallas_call x1, Pallas kernels, per_device(): call(spectrum_kernel, (shape((rows, 2 * tokens), F32), shape((tokens, wid...  2.5 us
  transfers between devices with their start and end apart: 7, of which 5 were waited for; matrix products, arithmetic and copies ran while one was open for 1% of the time, Pallas kernels for 14%

profile of v6, /device:TPU:6, one launch (start us, length us, event | category | flops | bytes accessed | tf_op | source)
XLA Modules:
  0.0 94.4 jit_solution(5305912185844430858)
XLA Ops:
  0.6 0.0 copy-start
  0.7 0.0 copy-start.5
  0.7 0.0 copy-start.6
  0.7 0.0 copy-start.7
  0.7 3.9 %shard_map.147 = bf16[64,40,128]{2,1,0:T(8,128)(2,1)} custom-call(s32[1,128]{1,0:T(1,128)} %ids_ref.3, bf16[512,2048]{1,0:T(8,128)(2,1)} %embed_hbm.5, bf16[128,2048]{1,0:T(8,128)(2,1)} %bitcast.9, bf16[32,2048]{1,0:T(8,128)(2,1)} %weight_hbm.1), custom_call_target="tpu_custom_call" | custom-call | flops 268435456 | bytes 5242880 | tf_op jit(solution)/shard_map/pallas_call | solution.py:619
  4.6 13.4 %all-to-all-start = ((bf16[64,40,128]{2,1,0:T(8,128)(2,1)}), bf16[64,40,128]{2,1,0:T(8,128)(2,1)}, u32[]{:S(2)}, u32[]{:S(2)}) async-start(bf16[64,40,128]{2,1,0:T(8,128)(2,1)} %shard_map.147), calls=%async_computation | async-start | bytes 1310720 | tf_op jit(solution)/shard_map/all_to_all | solution.py:599
  18.1 1.2 %copy-done.4 = f32[32,8192]{1,0:T(8,128)S(1)} copy-done((f32[32,8192]{1,0:T(8,128)S(1)}, f32[32,8192]{1,0:T(8,128)}, u32[]{:S(2)}) %copy-start.4) | copy-done | bytes 1048600
  19.3 2.5 %shard_map.148 = (f32[2048,256]{1,0:T(8,128)S(1)}, bf16[128,2048]{1,0:T(8,128)(2,1)S(1)}) custom-call(f32[32,8192]{1,0:T(8,128)S(1)} %copy-done.4, bf16[128,192]{1,0:T(8,128)(2,1)S(1)} %copy-done.7, f32[64,256]{1,0:T(8,128)S(1)} %copy-done.6, bf16[4,256,256]{2,1,0:T(8,128)(2,1)S(1)} %copy-done.5, s32[1,128]{1,0:T(1,128)S(1)} %copy-done.3, ...), custom_call_target="tpu_custom_call" | custom-call | flops 5368709120 | bytes 3145728 | tf_op jit(solution)/shard_map/pallas_call | solution.py:635
  21.8 1.3 %copy-done.8 = f32[2048,256]{1,0:T(8,128)} copy-done((f32[2048,256]{1,0:T(8,128)}, f32[2048,256]{1,0:T(8,128)S(1)}, u32[]{:S(2)}) %copy-start.8) | copy-done | bytes 2097176
  23.1 16.3 %all-to-all-done.block_ref = bf16[64,40,128]{2,1,0:T(8,128)(2,1)} async-done(((bf16[64,40,128]{2,1,0:T(8,128)(2,1)}), bf16[64,40,128]{2,1,0:T(8,128)(2,1)}, u32[]{:S(2)}, u32[]{:S(2)}) %all-to-all-start) | async-done | bytes 655392 | tf_op jit(solution)/shard_map/all_to_all | solution.py:599
  39.4 9.1 %shard_map.149 = (f32[64,8,128]{2,1,0:T(8,128)}, bf16[128,128]{1,0:T(8,128)(2,1)}, bf16[512,128]{1,0:T(8,128)(2,1)}) custom-call(bf16[64,40,128]{2,1,0:T(8,128)(2,1)} %all-to-all-done.block_ref, bf16[512,2048]{1,0:T(8,128)(2,1)} %embed_hbm.5, f32[2048,256]{1,0:T(8,128)} %copy-done.8, bf16[128,128]{1,0:T(8,128)(2,1)} %constant.18.clone.exact_hbm, ...), custom_call_target="tpu_custom_call" | custom-call | flops 10737418240 | bytes 6291456 | tf_op jit(solution)/shard_map/pallas_call | solution.py:649
  48.5 0.1 collective-permute-start
  48.6 5.1 %all-to-all-start.2 = ((f32[64,8,128]{2,1,0:T(8,128)}), f32[64,8,128]{2,1,0:T(8,128)S(1)}, u32[]{:S(2)}, u32[]{:S(2)}) async-start(f32[64,8,128]{2,1,0:T(8,128)} %get-tuple-element.16), calls=%async_computation.2 | async-start | bytes 524288 | tf_op jit(solution)/shard_map/all_to_all | solution.py:599
  53.7 0.6 copy-done.10
  54.3 8.6 %shard_map.150 = bf16[64,32,128]{2,1,0:T(8,128)(2,1)} custom-call(bf16[512,128]{1,0:T(8,128)(2,1)} %get-tuple-element.13.tails_hbm, bf16[128,128]{1,0:T(8,128)(2,1)} %copy-done.10, bf16[512,2048]{1,0:T(8,128)(2,1)} %embed_hbm.5, f32[2048,256]{1,0:T(8,128)} %copy-done.8, bf16[128,128]{1,0:T(8,128)(2,1)} %constant.18.clone.exact_hbm, ...), custom_call_target="tpu_custom_call" | custom-call | flops 10737418240 | bytes 6291456 | tf_op jit(solution)/shard_map/pallas_call | solution.py:675
  63.0 4.7 %all-to-all-done.2.grad_hbm = f32[64,8,128]{2,1,0:T(8,128)S(1)} async-done(((f32[64,8,128]{2,1,0:T(8,128)}), f32[64,8,128]{2,1,0:T(8,128)S(1)}, u32[]{:S(2)}, u32[]{:S(2)}) %all-to-all-start.2) | async-done | bytes 262176 | tf_op jit(solution)/shard_map/all_to_all | solution.py:599
  67.6 6.6 %all-to-all-start.1 = ((bf16[64,32,128]{2,1,0:T(8,128)(2,1)}), bf16[64,32,128]{2,1,0:T(8,128)(2,1)S(1)}, u32[]{:S(2)}, u32[]{:S(2)}) async-start(bf16[64,32,128]{2,1,0:T(8,128)(2,1)} %shard_map.150), calls=%async_computation.1 | async-start | bytes 1048576 | tf_op jit(solution)/shard_map/all_to_all | solution.py:599
  74.3 1.8 %shard_map.152 = (f32[32,2048]{1,0:T(8,128)}, f32[32,2048]{1,0:T(8,128)}, bf16[32,2048]{1,0:T(8,128)(2,1)S(1)}) custom-call(f32[64,8,128]{2,1,0:T(8,128)S(1)} %all-to-all-done.2.grad_hbm, f32[32,2048]{1,0:T(8,128)S(1)} %bitcast.6, f32[32,2048]{1,0:T(8,128)S(1)} %bitcast.7), custom_call_target="tpu_custom_call" | custom-call | flops 1048576 | bytes 2097152 | tf_op jit(solution)/shard_map/pallas_call | solution.py:697
  76.1 1.5 %collective-permute-start.2 = (bf16[32,2048]{1,0:T(8,128)(2,1)S(1)}, bf16[32,2048]{1,0:T(8,128)(2,1)S(1)}, u32[]{:S(2)}, u32[]{:S(2)}) collective-permute-start(bf16[32,2048]{1,0:T(8,128)(2,1)S(1)} %get-tuple-element.19), channel_id=1, source_target_pairs={{0,128},{64,192},{128,0},{192,64},{1,129},{65,193},{129,1},{193,65... | collective-permute-start | bytes 393224 | tf_op jit(solution)/shard_map/ppermute | solution.py:718
  77.6 6.8 %collective-permute-done.2 = bf16[32,2048]{1,0:T(8,128)(2,1)S(1)} collective-permute-done((bf16[32,2048]{1,0:T(8,128)(2,1)S(1)}, bf16[32,2048]{1,0:T(8,128)(2,1)S(1)}, u32[]{:S(2)}, u32[]{:S(2)}) %collective-permute-start.2) | collective-permute-done | bytes 131104 | tf_op jit(solution)/shard_map/ppermute | solution.py:718
  84.4 1.3 %collective-permute-done.3 = bf16[32,2048]{1,0:T(8,128)(2,1)S(1)} collective-permute-done((bf16[32,2048]{1,0:T(8,128)(2,1)S(1)}, bf16[32,2048]{1,0:T(8,128)(2,1)S(1)}, u32[]{:S(2)}, u32[]{:S(2)}) %collective-permute-start.3) | collective-permute-done | bytes 131104 | tf_op jit(solution)/shard_map/ppermute | solution.py:718
  85.7 0.8 subtract_convert_fusion
  86.5 6.7 %all-to-all-done.1.conv_ref = bf16[64,32,128]{2,1,0:T(8,128)(2,1)S(1)} async-done(((bf16[64,32,128]{2,1,0:T(8,128)(2,1)}), bf16[64,32,128]{2,1,0:T(8,128)(2,1)S(1)}, u32[]{:S(2)}, u32[]{:S(2)}) %all-to-all-start.1) | async-done | bytes 524320 | tf_op jit(solution)/shard_map/all_to_all | solution.py:599
  93.1 1.1 %shard_map.151 = bf16[128,2048]{1,0:T(8,128)(2,1)} custom-call(bf16[64,32,128]{2,1,0:T(8,128)(2,1)S(1)} %all-to-all-done.1.conv_ref, bf16[128,2048]{1,0:T(8,128)(2,1)S(1)} %get-tuple-element.15.inputs_hbm), custom_call_target="tpu_custom_call" | custom-call | flops 1048576 | bytes 2097152 | tf_op jit(solution)/shard_map/pallas_call | solution.py:727
  (19 shorter events, 0.0 us)
Async XLA Ops:
  0.6 17.4 %copy-start = (bf16[512,2048]{1,0:T(8,128)(2,1)S(1)}, bf16[512,2048]{1,0:T(8,128)(2,1)}, u32[]{:S(2)}) copy-start(bf16[512,2048]{1,0:T(8,128)(2,1)} %embed_hbm.5) | copy-start | bytes 6291460
  0.6 17.4 %copy-start.3 = (s32[1,128]{1,0:T(1,128)S(1)}, s32[1,128]{1,0:T(1,128)}, u32[]{:S(2)}) copy-start(s32[1,128]{1,0:T(1,128)} %ids_ref.3) | copy-start | bytes 1540
  0.7 17.4 %copy-start.5 = (bf16[4,256,256]{2,1,0:T(8,128)(2,1)S(1)}, bf16[4,256,256]{2,1,0:T(8,128)(2,1)}, u32[]{:S(2)}) copy-start(bf16[4,256,256]{2,1,0:T(8,128)(2,1)} %constant.17.clone.mix_ref.mix_hbm) | copy-start | bytes 1572868
  0.7 17.4 %copy-start.6 = (f32[64,256]{1,0:T(8,128)S(1)}, f32[64,256]{1,0:T(8,128)}, u32[]{:S(2)}) copy-start(f32[64,256]{1,0:T(8,128)} %constant.16.clone.twist_ref.twist_hbm) | copy-start | bytes 196612
  0.7 17.4 %copy-start.7 = (bf16[128,192]{1,0:T(8,128)(2,1)S(1)}, bf16[128,192]{1,0:T(8,128)(2,1)}, u32[]{:S(2)}) copy-start(bf16[128,192]{1,0:T(8,128)(2,1)} %constant.15.clone.wide_ref) | copy-start | bytes 147460
  4.6 34.8 %all-to-all-start = ((bf16[64,40,128]{2,1,0:T(8,128)(2,1)}), bf16[64,40,128]{2,1,0:T(8,128)(2,1)}, u32[]{:S(2)}, u32[]{:S(2)}) async-start(bf16[64,40,128]{2,1,0:T(8,128)(2,1)} %shard_map.147), calls=%async_computation | async-start | bytes 1310720 | tf_op jit(solution)/shard_map/all_to_all | solution.py:599
  18.0 1.2 %copy-start.4 = (f32[32,8192]{1,0:T(8,128)S(1)}, f32[32,8192]{1,0:T(8,128)}, u32[]{:S(2)}) copy-start(f32[32,8192]{1,0:T(8,128)} %filters_ref.1) | copy-start | bytes 3145732
  21.8 1.3 %copy-start.8 = (f32[2048,256]{1,0:T(8,128)}, f32[2048,256]{1,0:T(8,128)S(1)}, u32[]{:S(2)}) copy-start(f32[2048,256]{1,0:T(8,128)S(1)} %get-tuple-element.12.spectrum_hbm) | copy-start | bytes 6291460
  48.5 5.2 %collective-permute-start = (bf16[128,128]{1,0:T(8,128)(2,1)}, bf16[128,128]{1,0:T(8,128)(2,1)S(1)}, u32[]{:S(2)}, u32[]{:S(2)}) collective-permute-start(bf16[128,128]{1,0:T(8,128)(2,1)} %get-tuple-element.14), channel_id=1, source_target_pairs={{0,64},{64,0},{128,192},{192,128},{1,65},{65,1},{129,193},{193,129... | collective-permute-start | bytes 98312 | tf_op jit(solution)/shard_map/ppermute | solution.py:673
  48.6 19.0 %all-to-all-start.2 = ((f32[64,8,128]{2,1,0:T(8,128)}), f32[64,8,128]{2,1,0:T(8,128)S(1)}, u32[]{:S(2)}, u32[]{:S(2)}) async-start(f32[64,8,128]{2,1,0:T(8,128)} %get-tuple-element.16), calls=%async_computation.2 | async-start | bytes 524288 | tf_op jit(solution)/shard_map/all_to_all | solution.py:599
  53.7 0.6 copy-start.10
  54.3 20.0 %copy-start.1 = (f32[1,32,2048]{2,1,0:T(8,128)S(1)}, f32[1,32,2048]{2,1,0:T(8,128)}, u32[]{:S(2)}) copy-start(f32[1,32,2048]{2,1,0:T(8,128)} %param.17) | copy-start | bytes 786436
  54.3 20.0 %copy-start.2 = (f32[1,32,2048]{2,1,0:T(8,128)S(1)}, f32[1,32,2048]{2,1,0:T(8,128)}, u32[]{:S(2)}) copy-start(f32[1,32,2048]{2,1,0:T(8,128)} %param.18) | copy-start | bytes 786436
  54.3 31.4 %copy-start.9 = (bf16[32,2048]{1,0:T(8,128)(2,1)S(1)}, bf16[32,2048]{1,0:T(8,128)(2,1)}, u32[]{:S(2)}) copy-start(bf16[32,2048]{1,0:T(8,128)(2,1)} %weight_hbm.1) | copy-start | bytes 393220
  67.6 25.5 %all-to-all-start.1 = ((bf16[64,32,128]{2,1,0:T(8,128)(2,1)}), bf16[64,32,128]{2,1,0:T(8,128)(2,1)S(1)}, u32[]{:S(2)}, u32[]{:S(2)}) async-start(bf16[64,32,128]{2,1,0:T(8,128)(2,1)} %shard_map.150), calls=%async_computation.1 | async-start | bytes 1048576 | tf_op jit(solution)/shard_map/all_to_all | solution.py:599
  76.1 8.2 %collective-permute-start.2 = (bf16[32,2048]{1,0:T(8,128)(2,1)S(1)}, bf16[32,2048]{1,0:T(8,128)(2,1)S(1)}, u32[]{:S(2)}, u32[]{:S(2)}) collective-permute-start(bf16[32,2048]{1,0:T(8,128)(2,1)S(1)} %get-tuple-element.19), channel_id=1, source_target_pairs={{0,128},{64,192},{128,0},{192,64},{1,129},{65,193},{129,1},{193,65... | collective-permute-start | bytes 393224 | tf_op jit(solution)/shard_map/ppermute | solution.py:718
  77.6 6.8 %collective-permute-start.1 = (bf16[32,2048]{1,0:T(8,128)(2,1)S(1)}, bf16[32,2048]{1,0:T(8,128)(2,1)S(1)}, u32[]{:S(2)}, u32[]{:S(2)}) collective-permute-start(bf16[32,2048]{1,0:T(8,128)(2,1)S(1)} %get-tuple-element.19), channel_id=1, source_target_pairs={{0,64},{64,0},{128,192},{192,128},{1,65},{65,1},{129,193},{193,129... | collective-permute-start | bytes 393224 | tf_op jit(solution)/shard_map/ppermute | solution.py:718
  84.4 1.3 %collective-permute-start.3 = (bf16[32,2048]{1,0:T(8,128)(2,1)S(1)}, bf16[32,2048]{1,0:T(8,128)(2,1)S(1)}, u32[]{:S(2)}, u32[]{:S(2)}) collective-permute-start(bf16[32,2048]{1,0:T(8,128)(2,1)S(1)} %collective-permute-done.2), channel_id=1, source_target_pairs={{0,64},{64,0},{128,192},{192,128},{1,65},{65,1},{129,193},{193,129... | collective-permute-start | bytes 393224 | tf_op jit(solution)/shard_map/ppermute | solution.py:718
